TPU v7x, 256 devices: a whole 4x4x8 slice. The times are simulated.
256 devices in a mesh: dp: 32 (over y, x, z_lo), layer: 8 (over z_hi, core).
Axes of the slice: x: 4, y: 4, z: 8 (z_hi: 4, z_lo: 2; z = z_hi * 2 + z_lo), core: 2. Of those that a mesh axis runs over, the one named last changes fastest.
Arguments:
- layer_inputs: bfloat16 [8, 32768, 4096], P('layer', 'dp'), may hold values from -6 to 6
- output_grads: bfloat16 [8, 32768, 512], P('layer', 'dp'), may hold values from -6 to 6
- input_factors: bfloat16 [256, 8, 4, 4096], P('dp', 'layer'), may hold values from -0.09375 to 0.09375
- output_factors: bfloat16 [256, 8, 4, 512], P('dp', 'layer'), may hold values from -0.25 to 0.25
Outputs:
- scores: float32 [256, 32768], P(None, 'dp')
All inputs are finite; a program needn't handle non-finite values.
Results may differ from a plain program's by a relative error of at most 0.0003.
Values may be sent and summed in bfloat16 or wider, within the bound.
No kernel may reach another device: no remote copies, remote signals or barrier semaphores. Data moves between devices by JAX's collectives and lax.ppermute only.
A program may use at most 128 MiB of HBM per device.

v0:
```python
import jax
import jax.numpy as jnp
from jax import lax
from jax.sharding import PartitionSpec as P


def in_one_piece(arrays, axis, dim, along):
    ends, at = ([], 0)
    for a in arrays[:-1]:
        at += a.shape[along]
        ends.append(at)
    both = jnp.concatenate(arrays, axis=along)
    return tuple(jnp.split(lax.all_gather(both, axis, axis=dim, tiled=True), ends, axis=along))


def split_up(value, dim, length):
    lengths = value.shape
    parts = value.reshape(*lengths[:dim], length, lengths[dim] // length, *lengths[dim + 1 :])
    return jnp.moveaxis(parts, dim, 0)


def sent_and_summed(value, axis, dim):
    length = lax.axis_size(axis)
    parts = lax.all_to_all(split_up(value, dim, length), axis, 0, 0, tiled=True)
    return jnp.sum(parts, axis=0)


def layer_term(acts, grads, in_fac, out_fac):
    count = in_fac.shape[0]
    in_flat = in_fac.reshape(count * in_fac.shape[1], in_fac.shape[2])
    out_flat = out_fac.reshape(count * out_fac.shape[1], out_fac.shape[2])
    proj_in = lax.dot_general(
        acts, in_flat, (((1,), (1,)), ((), ())), preferred_element_type=jnp.float32
    )
    proj_out = lax.dot_general(
        grads, out_flat, (((1,), (1,)), ((), ())), preferred_element_type=jnp.float32
    )
    joined = (proj_in * proj_out).reshape(acts.shape[0], count, in_fac.shape[1])
    return jnp.sum(joined, axis=2).T


def local_scores(layer_inputs, output_grads, in_piece, out_piece):
    term = layer_term(layer_inputs[0], output_grads[0], in_piece[:, 0], out_piece[:, 0])
    return term


def shards(layer_inputs, output_grads, input_factors, output_factors):
    in_all, out_all = in_one_piece((input_factors, output_factors), "dp", 0, 3)
    partial_scores = local_scores(layer_inputs, output_grads, in_all, out_all)
    share = sent_and_summed(partial_scores, "layer", 0)
    return lax.all_gather(share, "layer", axis=0, tiled=True)


def solution(mesh):
    in_specs = (
        P("layer", "dp", None),
        P("layer", "dp", None),
        P("dp", "layer", None, None),
        P("dp", "layer", None, None),
    )
    out_specs = P(None, "dp")
    return jax.shard_map(shards, mesh=mesh, in_specs=in_specs, out_specs=out_specs, check_vma=False)
```

profile of v0, /device:TPU:1, one launch (start us, length us, event | category | flops | bytes accessed | tf_op | source)
XLA Modules:
  0.0 343.2 jit_solution(17840283260817225052)
XLA Ops:
  6.5 0.0 copy-start
  6.5 0.0 all-gather.3.cloned.1.call-start
  6.5 1.9 pad_maximum_fusion
  8.4 0.0 all-gather.3.cloned.1.call-update
  8.5 0.0 all-gather.5.cloned.1.call-start
  8.5 218.6 %all-gather.3.cloned.1.call-done = bf16[256,1,4,4608]{3,2,1,0:T(4,128)(2,1)} async-done(((bf16[8,1,4,4608]{3,2,1,0:T(4,128)(2,1)}), bf16[256,1,4,4608]{3,2,1,0:T(4,128)(2,1)}) %all-gather.3.cloned.1.call-update) | async-done | bytes 9437200 | tf_op jit(solution)/shard_map/all_gather | solution.py:13
  227.1 8.6 %split.8 = bf16[256,1,4,4096]{3,2,1,0:T(4,128)(2,1)} slice(bf16[256,1,4,4608]{3,2,1,0:T(4,128)(2,1)} %all-gather.3.cloned.1.call-done), slice={[0:256], [0:1], [0:4], [0:4096]} | slice | bytes 16777216 | tf_op jit(solution)/shard_map/split | solution.py:13
  235.7 0.0 slice-start
  235.7 12.6 %reshape_squeeze.6 = bf16[1024,4096]{1,0:T(8,128)(2,1)} reshape(bf16[256,1,4,4096]{3,2,1,0:T(4,128)(2,1)} %split.8) | data formatting | bytes 16777216 | tf_op jit(solution)/shard_map/reshape;squeeze | solution.py:30
  248.3 0.0 slice-done
  248.3 0.3 reshape_squeeze.7
  248.6 0.0 copy-done
  248.6 0.0 copy-start.1
  248.6 1.3 fusion.4
  249.9 2.1 copy-done.1
  252.0 12.6 %multiply_bitcast_fusion = f32[1024,1024]{0,1:T(8,128)} fusion(f32[1024,1024]{1,0:T(8,128)S(1)} %fusion.4, bf16[1024,4096]{1,0:T(8,128)(2,1)S(1)} %copy-done.1, bf16[1,1024,4096]{2,1,0:T(8,128)(2,1)} %param.4), kind=kOutput, calls=%fused_computation.2 | convolution fusion | flops 8590983168 | bytes 25165824 | tf_op jit(solution)/shard_map/dot_general | solution.py:32
  264.5 5.2 %reshape.6 = f32[1024,256,4]{0,2,1:T(4,128)} reshape(f32[1024,1024]{0,1:T(8,128)} %multiply_bitcast_fusion) | data formatting | bytes 8388608 | tf_op jit(solution)/shard_map/reshape | solution.py:38
  269.7 4.7 %reduce_sum.18 = f32[1024,256]{0,1:T(8,128)S(1)} reduce(f32[1024,256,4]{0,2,1:T(4,128)} %reshape.6, f32[]{:T(128)} %constant.0.clone.1), dimensions={2}, to_apply=%region_0.0 | reduce | flops 786432 | bytes 5242884 | tf_op jit(solution)/shard_map/reduce_sum | solution.py:39
  274.5 32.9 %all_to_all.5 = f32[8,32,1024]{2,1,0:T(8,128)S(1)} all-to-all(f32[8,32,1024]{2,1,0:T(8,128)S(1)} %bitcast.17), channel_id=1, replica_groups=mesh['dp'=32,'layer'=8] {'layer'}, dimensions={0} | all-to-all | bytes 2097152 | tf_op jit(solution)/shard_map/all_to_all | solution.py:24
  307.4 0.7 reduce_sum.19
  308.1 0.0 all-gather.5.cloned.1.call-update
  308.1 25.9 %all-gather.5.cloned.1.call-done = f32[256,1024]{1,0:T(8,128)} async-done(((f32[32,1024]{1,0:T(8,128)}), f32[256,1024]{1,0:T(8,128)}) %all-gather.5.cloned.1.call-update) | async-done | bytes 1048592 | tf_op jit(solution)/shard_map/all_gather | solution.py:51
  334.0 2.3 copy.6
Async XLA Ops:
  6.5 242.0 %copy-start = (bf16[1,1024,512]{2,1,0:T(8,128)(2,1)S(1)}, bf16[1,1024,512]{2,1,0:T(8,128)(2,1)}, u32[]{:S(2)}) copy-start(bf16[1,1024,512]{2,1,0:T(8,128)(2,1)} %param.5) | copy-start | bytes 3145732
  6.5 220.6 %all-gather.3.cloned.1.call-start = ((), (), s32[]{:S(2)}) async-start(), calls=%async_computation.1 | async-start | bytes 9732096 | tf_op jit(solution)/shard_map/all_gather | solution.py:13
  8.5 325.5 %all-gather.5.cloned.1.call-start = ((), (), s32[]{:S(2)}) async-start(), calls=%async_computation.2 | async-start | bytes 1179648 | tf_op jit(solution)/shard_map/all_gather | solution.py:51
  235.7 12.6 %slice-start = ((bf16[256,1,4,4608]{3,2,1,0:T(4,128)(2,1)}), bf16[256,1,4,512]{3,2,1,0:T(4,128)(2,1)S(1)}, s32[]{:S(2)}) async-start(bf16[256,1,4,4608]{3,2,1,0:T(4,128)(2,1)} %all-gather.3.cloned.1.call-done), calls=%async_computation.3 | async-start | bytes 2097152 | tf_op jit(solution)/shard_map/split | solution.py:13
  248.6 3.4 copy-start.1
Sparse Core Ops, SparseCore 0:
  9.1 217.9 all-gather.2
  308.2 25.7 all-gather.4
where the time goes:
time: 344 us; the launch traced here: 343 us
  waiting for transfers between devices  245 us (71%)
  blocking collectives  32.9 us (10%)
  local copies, waits for them, and re-layouts  31 us (9%)
  matrix products  13.9 us (4%)
  between operations  13.4 us (4%)
  other arithmetic  7.36 us (2%)
    all_gather x1, waiting for transfers between devices, in_one_piece(): lax.all_gather(both, axis, axis=dim, tiled=True)  219 us
    all_to_all x1, blocking collectives, sent_and_summed(): parts = lax.all_to_all(split_up(value, dim, length), axis, 0, 0, tiled=True)  32.9 us
    all_gather x1, waiting for transfers between devices, shards(): return lax.all_gather(share, 'layer', axis=0, tiled=True)  25.9 us
    another operation x1, local copies, waits for them, and re-layouts, layer_term(): in_flat = in_fac.reshape(count * in_fac.shape[1], in_fac.shape[2])  12.6 us
    dot_general x1, matrix products, layer_term(): lax.dot_general(acts, in_flat, (((1,), (1,)), ((), ())), preferred_elemen...  12.6 us
    split x3, local copies, waits for them, and re-layouts, in_one_piece(): jnp.split(lax.all_gather(both, axis, axis=dim, tiled=True), ends, axis=al...  8.56 us
  transfers between devices with their start and end apart: 2, of which 2 were waited for; matrix products, arithmetic and copies ran while one was open for 0% of the time, Pallas kernels for 0%

commit v1 on v0

v1 whole, which is shorter than its diff:
```python
import functools

import jax
import jax.numpy as jnp
from jax import lax
from jax.experimental import pallas as pl
from jax.experimental.pallas import tpu as pltpu
from jax.sharding import PartitionSpec as P

NY, NX, NZ = 4, 4, 2
RANK = 4
QPD = 8
ROWS = RANK * QPD
HALF = ROWS // 2
TB = 256


def dp_of(y, x, z):
    return ((y % NY) * NX + x % NX) * NZ + z % NZ


def dp_perm(dy, dx, dz):
    return [
        (dp_of(y, x, z), dp_of(y + dy, x + dx, z + dz))
        for y in range(NY)
        for x in range(NX)
        for z in range(NZ)
    ]


STEPS = {
    "XP": dp_perm(0, 1, 0),
    "XM": dp_perm(0, -1, 0),
    "YP": dp_perm(1, 0, 0),
    "YM": dp_perm(-1, 0, 0),
    "Z": dp_perm(0, 0, 1),
}
MOVE = {"XP": (0, -1, 0), "XM": (0, 1, 0), "YP": (0, 0, -1), "YM": (0, 0, 1), "Z": (1, 0, 0)}
CORE_SWAP = [(i, i ^ 1) for i in range(8)]


def layer_pairs(first):
    out = []
    for zh in range(4):
        for core in range(2):
            even = core == first
            other = zh ^ 1 if even else ((zh + 1) % 4 if zh % 2 == 1 else (zh - 1) % 4)
            out.append((zh * 2 + core, other * 2 + core))
    return out


PAIR_A, PAIR_B = layer_pairs(0), layer_pairs(1)


def wrap(d):
    return (d + 1) % 4 - 1


def moved(piece, step):
    plane, dx, dy, part = piece
    mz, mx, my = MOVE[step]
    return (plane ^ mz, wrap(dx + mx), wrap(dy + my), part)


def piece_rows(piece):
    return ROWS if piece[3] is None else HALF


class Pieces:
    def __init__(self, own):
        self.where = {(0, 0, 0, None): (own, 0)}

    def get(self, piece):
        if piece in self.where:
            buf, at = self.where[piece]
            n = piece_rows(piece)
            return buf if buf.shape[0] == n else lax.slice_in_dim(buf, at, at + n, axis=0)
        whole = piece[:3] + (None,)
        if whole in self.where:
            buf, at = self.where[whole]
            at += piece[3] * HALF
            return lax.slice_in_dim(buf, at, at + HALF, axis=0)
        return jnp.concatenate([self.get(piece[:3] + (h,)) for h in (0, 1)], axis=0)

    def send(self, step, pieces):
        parts = [self.get(p) for p in pieces]
        data = parts[0] if len(parts) == 1 else jnp.concatenate(parts, axis=0)
        got = lax.ppermute(data, "dp", STEPS[step])
        at, names = 0, []
        for p in pieces:
            q = moved(p, step)
            self.where[q] = (got, at)
            names.append(q)
            at += piece_rows(q)
        return got, names


def term_kernel(n_buf, plan, blocks, x_ref, g_ref, *refs):
    bufs, out_ref, fac = refs[:n_buf], refs[n_buf], refs[n_buf + 1]
    core = lax.rem(lax.axis_index("layer"), 2)
    at = 0
    for b in bufs:
        fac[at : at + b.shape[0], :] = b[...]
        at += b.shape[0]
    depth = x_ref.shape[1]
    half = len(blocks) // 2

    @pl.loop(0, x_ref.shape[0] // TB)
    def _(i):
        t = pl.multiple_of(i * TB, TB)
        dims = (((1,), (1,)), ((), ()))
        a = lax.dot_general(
            fac[:, :depth], x_ref[pl.ds(t, TB), :], dims, preferred_element_type=jnp.float32
        )
        b = lax.dot_general(
            fac[:, depth:], g_ref[pl.ds(t, TB), :], dims, preferred_element_type=jnp.float32
        )
        c = a * b
        for k, block in enumerate(blocks):
            tiles = [c[r : r + QPD, :] for r in plan[block]]
            total = (tiles[0] + tiles[1]) + (tiles[2] + tiles[3])
            h, row = divmod(k, half)
            which = jnp.bitwise_xor(core, h)
            out_ref[which, row * QPD : (row + 1) * QPD, pl.ds(t, TB)] = total


def term(x, g, received):
    plan, at = {}, 0
    for _, names in received:
        for name in names:
            n = piece_rows(name)
            plan.setdefault(name[:3], []).extend(range(at, at + n, QPD))
            at += n
    blocks = sorted(plan)
    assert all(len(v) == RANK for v in plan.values()) and len(blocks) % 2 == 0
    vmem = pl.BlockSpec(memory_space=pltpu.VMEM)
    tokens, width = x.shape[0], x.shape[1] + g.shape[1]
    out = pl.pallas_call(
        functools.partial(term_kernel, len(received), plan, blocks),
        out_shape=jax.ShapeDtypeStruct((2, len(blocks) // 2 * QPD, tokens), jnp.float32),
        in_specs=[vmem] * (2 + len(received)),
        out_specs=vmem,
        scratch_shapes=[pltpu.VMEM((at, width), jnp.bfloat16)],
        compiler_params=pltpu.CompilerParams(vmem_limit_bytes=20 * 2**20),
        cost_estimate=pl.CostEstimate(
            flops=2 * at * width * tokens, bytes_accessed=at * width * 2, transcendentals=0
        ),
    )(x, g, *[b for b, _ in received])
    return out, blocks


def layer_sum(terms):
    keep = [t[0] for t in terms]
    send = [t[1] for t in terms]
    keep = keep[0] if len(keep) == 1 else jnp.concatenate(keep, axis=0)
    send = send[0] if len(send) == 1 else jnp.concatenate(send, axis=0)
    mine = keep + lax.ppermute(send, "layer", CORE_SWAP)
    mine = mine + lax.ppermute(mine, "layer", PAIR_A)
    mine = mine + lax.ppermute(mine, "layer", PAIR_B)
    return mine, lax.ppermute(mine, "layer", CORE_SWAP)


def place_kernel(groups, *refs):
    out_ref = refs[-1]
    core = lax.rem(lax.axis_index("layer"), 2)
    d = lax.axis_index("dp")
    z, x, y = lax.rem(d, NZ), lax.rem(d // NZ, NX), d // (NZ * NX)
    for g, halves in enumerate(groups):
        for h in range(2):
            for row, (plane, dx, dy) in enumerate(halves[h]):
                at = ((lax.rem(y + dy + NY, NY) * NX + lax.rem(x + dx + NX, NX)) * NZ
                      + jnp.bitwise_xor(z, plane)) * QPD
                rows = pl.ds(row * QPD, QPD)
                mine, other = refs[2 * g], refs[2 * g + 1]

                @pl.when(core == h)
                def _():
                    out_ref[pl.ds(pl.multiple_of(at, QPD), QPD), :] = mine[rows, :]

                @pl.when(core != h)
                def _():
                    out_ref[pl.ds(pl.multiple_of(at, QPD), QPD), :] = other[rows, :]


def place(groups, arrays, queries):
    vmem = pl.BlockSpec(memory_space=pltpu.VMEM)
    return pl.pallas_call(
        functools.partial(place_kernel, groups),
        out_shape=jax.ShapeDtypeStruct((queries, arrays[0].shape[1]), jnp.float32),
        in_specs=[vmem] * len(arrays),
        out_specs=vmem,
        compiler_params=pltpu.CompilerParams(vmem_limit_bytes=12 * 2**20),
    )(*arrays)


def shards(layer_inputs, output_grads, input_factors, output_factors):
    x, g = layer_inputs[0], output_grads[0]
    own = jnp.concatenate([input_factors[:, 0], output_factors[:, 0]], axis=2)
    own = jnp.swapaxes(own, 0, 1).reshape(ROWS, own.shape[2])
    have = Pieces(own)
    A, B = 0, 1
    rz = have.send("Z", [(A, 0, 0, None)])
    first = [have.send(s, [(A, 0, 0, None)]) for s in ("XP", "XM", "YP", "YM")]
    c0 = [(own, [(A, 0, 0, None)]), rz] + first
    c1 = [
        have.send("XP", [(A, -1, 0, 1), (B, 0, 0, None)]),
        have.send("XM", [(A, 1, 0, 0), (B, 0, 0, None)]),
        have.send("YP", [(A, 0, -1, 1), (B, 0, 0, None)]),
        have.send("YM", [(A, 0, 1, 0), (B, 0, 0, None)]),
    ]
    c2 = [have.send(s, [(A, 1, 0, None), (A, -1, 0, None)]) for s in ("YP", "YM")]
    c3 = [
        have.send("XP", [(B, -1, 0, 1), (B, 0, 1, None), (B, 0, -1, None)]),
        have.send("XM", [(B, 1, 0, 0), (B, 0, 1, None), (B, 0, -1, None)]),
        have.send("YP", [(B, 0, -1, 1), (A, 2, 0, None)]),
        have.send("YM", [(B, 0, 1, 0), (A, 2, 0, None)]),
    ]
    c4 = [
        have.send("XP", [(B, -1, 1, 1), (B, -1, -1, 1)]),
        have.send("XM", [(B, 1, 1, 0), (B, 1, -1, 0)]),
        have.send("YP", [(A, 1, -1, 1), (A, -1, -1, 1)]),
        have.send("YM", [(A, 1, 1, 0), (A, -1, 1, 0)]),
        have.send("XP", [(B, 0, 2, None)]),
        have.send("XM", [(B, 0, 2, None)]),
    ]
    c5 = [
        have.send("YP", [(A, 2, -1, 1)]),
        have.send("YM", [(A, 2, 1, 0)]),
        have.send("XP", [(B, -1, 2, 1)]),
        have.send("XM", [(B, 1, 2, 0)]),
    ]
    groups, arrays = [], []
    for chunks in ((c0, c1), (c2, c3), (c4, c5)):
        terms, halves = [], ([], [])
        for c in chunks:
            out, blocks = term(x, g, c)
            terms.append(out)
            halves[0].extend(blocks[: len(blocks) // 2])
            halves[1].extend(blocks[len(blocks) // 2 :])
        arrays.extend(layer_sum(terms))
        groups.append(halves)
    return place(groups, arrays, lax.axis_size("dp") * QPD)


def solution(mesh):
    in_specs = (
        P("layer", "dp", None),
        P("layer", "dp", None),
        P("dp", "layer", None, None),
        P("dp", "layer", None, None),
    )
    out_specs = P(None, "dp")
    return jax.shard_map(shards, mesh=mesh, in_specs=in_specs, out_specs=out_specs, check_vma=False)
```

time: 344 us -> 119 us (0.35)
  waiting for transfers between devices: 245 us -> 27.9 us
  starting transfers between devices: 0.04 us -> 60.8 us
  blocking collectives: 32.9 us -> 0 us
  local copies, waits for them, and re-layouts: 31 us -> 4.71 us
  Pallas kernels: 0 us -> 23.3 us
  matrix products: 13.9 us -> 0 us
  between operations: 13.4 us -> 0.62 us
  other arithmetic: 7.36 us -> 1.75 us
    all_gather x2 -> x0, waiting for transfers between devices: 245 us -> none  [the longest x1 219 us: in_one_piece(): lax.all_gather(both, axis, axis=dim, tiled=True)]
    ppermute x0 -> x37, starting transfers between devices: none -> 60.8 us  [the longest x25 32 us: send(): got = lax.ppermute(data, 'dp', STEPS[step])]
    all_to_all x1 -> x0, blocking collectives: 32.9 us -> none  [sent_and_summed(): parts = lax.all_to_all(split_up(value, dim, length), axis, 0, 0, tiled=True)]
    ppermute x0 -> x37, waiting for transfers between devices: none -> 27.9 us  [the longest x25 17 us: send(): got = lax.ppermute(data, 'dp', STEPS[step])]
    pallas_call x0 -> x7, Pallas kernels: none -> 23.3 us  [the longest x6 22.1 us: term(): pl.pallas_call(functools.partial(term_kernel, len(received), plan, blocks...]
    dot_general x2 -> x0, matrix products: 13.9 us -> none  [the longest x1 12.6 us: layer_term(): lax.dot_general(acts, in_flat, (((1,), (1,)), ((), ())), preferred_elemen...]
    another operation x2 -> x0, local copies, waits for them, and re-layouts: 12.9 us -> none  [the longest x1 12.6 us: layer_term(): in_flat = in_fac.reshape(count * in_fac.shape[1], in_fac.shape[2])]
    split x3 -> x0, local copies, waits for them, and re-layouts: 8.56 us -> none  [in_one_piece(): jnp.split(lax.all_gather(both, axis, axis=dim, tiled=True), ends, axis=al...]
  transfers between devices with their start and end apart: 2 -> 37, of which waited for: 2 -> 11; matrix products, arithmetic and copies ran while one was open for 0% -> 1% of each run, Pallas kernels for 0% -> 19%
where the time goes in v1:
time: 119 us
  starting transfers between devices  60.8 us (51%)
  waiting for transfers between devices  27.9 us (23%)
  Pallas kernels  23.3 us (20%)
  local copies, waits for them, and re-layouts  4.71 us (4%)
  other arithmetic  1.75 us (1%)
    ppermute x25, starting transfers between devices, send(): got = lax.ppermute(data, 'dp', STEPS[step])  32 us
    pallas_call x6, Pallas kernels, term(): pl.pallas_call(functools.partial(term_kernel, len(received), plan, blocks...  22.1 us
    ppermute x25, waiting for transfers between devices, send(): got = lax.ppermute(data, 'dp', STEPS[step])  17 us
    ppermute x3, starting transfers between devices, layer_sum(): mine = mine + lax.ppermute(mine, 'layer', PAIR_A)  10.6 us
    ppermute x3, starting transfers between devices, layer_sum(): mine = mine + lax.ppermute(mine, 'layer', PAIR_B)  8.91 us
    ppermute x3, starting transfers between devices, layer_sum(): mine = keep + lax.ppermute(send, 'layer', CORE_SWAP)  8.55 us
    ppermute x3, waiting for transfers between devices, layer_sum(): mine = mine + lax.ppermute(mine, 'layer', PAIR_A)  7.06 us
    unnamed x7, local copies, waits for them, and re-layouts  3.41 us
  transfers between devices with their start and end apart: 37, of which 11 were waited for; matrix products, arithmetic and copies ran while one was open for 1% of the time, Pallas kernels for 19%

profile of v1, /device:TPU:1, one launch (start us, length us, event | category | flops | bytes accessed | tf_op | source)
XLA Modules:
  0.0 119.2 jit_solution(4451597868524786917)
XLA Ops:
  1.2 3.6 %collective-permute-start.4 = (bf16[32,4608]{1,0:T(8,128)(2,1)S(1)}, bf16[32,4608]{1,0:T(8,128)(2,1)S(1)}, u32[]{:S(2)}, u32[]{:S(2)}) collective-permute-start(bf16[32,4608]{1,0:T(8,128)(2,1)S(1)} %bitcast.45), channel_id=1, source_target_pairs={{0,192},{8,200},{16,208},{24,216},{32,224},{40,232},{48,240},{56,2... | collective-permute-start | bytes 884744 | tf_op jit(solution)/shard_map/ppermute | solution.py:88
  4.8 2.5 %collective-permute-start.2 = (bf16[32,4608]{1,0:T(8,128)(2,1)S(1)}, bf16[32,4608]{1,0:T(8,128)(2,1)S(1)}, u32[]{:S(2)}, u32[]{:S(2)}) collective-permute-start(bf16[32,4608]{1,0:T(8,128)(2,1)S(1)} %bitcast.46), channel_id=1, source_target_pairs={{0,48},{8,56},{16,0},{24,8},{32,16},{40,24},{48,32},{56,40},{64,11... | collective-permute-start | bytes 884744 | tf_op jit(solution)/shard_map/ppermute | solution.py:88
  10.5 2.1 %collective-permute-done.2.refs_3_ = bf16[32,4608]{1,0:T(8,128)(2,1)S(1)} collective-permute-done((bf16[32,4608]{1,0:T(8,128)(2,1)S(1)}, bf16[32,4608]{1,0:T(8,128)(2,1)S(1)}, u32[]{:S(2)}, u32[]{:S(2)}) %collective-permute-start.2) | collective-permute-done | bytes 294944 | tf_op jit(solution)/shard_map/ppermute | solution.py:88
  12.7 3.1 %collective-permute-done.3.refs_4_ = bf16[32,4608]{1,0:T(8,128)(2,1)S(1)} collective-permute-done((bf16[32,4608]{1,0:T(8,128)(2,1)S(1)}, bf16[32,4608]{1,0:T(8,128)(2,1)S(1)}, u32[]{:S(2)}, u32[]{:S(2)}) %collective-permute-start.3) | collective-permute-done | bytes 294944 | tf_op jit(solution)/shard_map/ppermute | solution.py:88
  16.1 2.7 %collective-permute-start.6 = (bf16[48,4608]{1,0:T(8,128)(2,1)S(1)}, bf16[48,4608]{1,0:T(8,128)(2,1)S(1)}, u32[]{:S(2)}, u32[]{:S(2)}) collective-permute-start(bf16[48,4608]{1,0:T(8,128)(2,1)S(1)} %get-tuple-element.26), channel_id=1, source_target_pairs={{0,48},{8,56},{16,0},{24,8},{32,16},{40,24},{48,32},{56,40},{64,11... | collective-permute-start | bytes 1327112 | tf_op jit(solution)/shard_map/ppermute | solution.py:88
  18.7 2.7 %collective-permute-start.8 = (bf16[48,4608]{1,0:T(8,128)(2,1)S(1)}, bf16[48,4608]{1,0:T(8,128)(2,1)S(1)}, u32[]{:S(2)}, u32[]{:S(2)}) collective-permute-start(bf16[48,4608]{1,0:T(8,128)(2,1)S(1)} %get-tuple-element.25), channel_id=1, source_target_pairs={{0,192},{8,200},{16,208},{24,216},{32,224},{40,232},{48,240},{56,2... | collective-permute-start | bytes 1327112 | tf_op jit(solution)/shard_map/ppermute | solution.py:88
  21.6 3.4 %copy-done = bf16[1,1024,4096]{2,1,0:T(8,128)(2,1)S(1)} copy-done((bf16[1,1024,4096]{2,1,0:T(8,128)(2,1)S(1)}, bf16[1,1024,4096]{2,1,0:T(8,128)(2,1)}, u32[]{:S(2)}) %copy-start) | copy-done | bytes 8388632
  24.9 3.8 %shard_map.46 = f32[2,24,1024]{2,1,0:T(8,128)S(1)} custom-call(bf16[1024,4096]{1,0:T(8,128)(2,1)S(1)} %bitcast.33, bf16[1024,512]{1,0:T(8,128)(2,1)S(1)} %bitcast.39, bf16[32,4608]{1,0:T(8,128)(2,1)S(1)} %bitcast.50, bf16[32,4608]{1,0:T(8,128)(2,1)S(1)} %collective-permute-done.refs_1_, bf16[32,4608]{1,0:T(8,128)(2,1)S(1)} %collective-permute-done.1.refs_2_, ...), custom_call_target="tpu_custom_call" | custom-call | flops 1811939328 | bytes 1769472 | tf_op jit(solution)/shard_map/pallas_call | solution.py:138
  28.8 2.7 %collective-permute-start.14 = (bf16[64,4608]{1,0:T(8,128)(2,1)S(1)}, bf16[64,4608]{1,0:T(8,128)(2,1)S(1)}, u32[]{:S(2)}, u32[]{:S(2)}) collective-permute-start(bf16[64,4608]{1,0:T(8,128)(2,1)S(1)} %constant_dynamic-update-slice_fusion), channel_id=1, source_target_pairs={{0,192},{8,200},{16,208},{24,216},{32,224},{40,232},{48,240},{56,2... | collective-permute-start | bytes 1769480 | tf_op jit(solution)/shard_map/ppermute | solution.py:88
  31.6 3.9 %shard_map.47 = f32[2,24,1024]{2,1,0:T(8,128)S(1)} custom-call(bf16[1024,4096]{1,0:T(8,128)(2,1)S(1)} %bitcast.34, bf16[1024,512]{1,0:T(8,128)(2,1)S(1)} %bitcast.40, bf16[48,4608]{1,0:T(8,128)(2,1)S(1)} %collective-permute-done.5.refs_0_, bf16[48,4608]{1,0:T(8,128)(2,1)S(1)} %collective-permute-done.6.refs_1_, ...), custom_call_target="tpu_custom_call" | custom-call | flops 1811939328 | bytes 1769472 | tf_op jit(solution)/shard_map/pallas_call | solution.py:138
  35.5 4.3 %collective-permute-start.9 = (f32[48,1024]{1,0:T(8,128)S(1)}, f32[48,1024]{1,0:T(8,128)S(1)}, u32[]{:S(2)}, u32[]{:S(2)}) collective-permute-start(f32[48,1024]{1,0:T(8,128)S(1)} %pad_maximum_fusion.17), channel_id=1, source_target_pairs={{0,1},{1,0},{2,3},{3,2},{4,5},{5,4},{6,7},{7,6},{8,9},{9,8},{10,11... | collective-permute-start | bytes 589832 | tf_op jit(solution)/shard_map/ppermute | solution.py:157
  40.9 2.7 %collective-permute-start.16 = (bf16[80,4608]{1,0:T(8,128)(2,1)S(1)}, bf16[80,4608]{1,0:T(8,128)(2,1)S(1)}, u32[]{:S(2)}, u32[]{:S(2)}) collective-permute-start(bf16[80,4608]{1,0:T(8,128)(2,1)S(1)} %get-tuple-element.13), channel_id=1, source_target_pairs={{0,48},{8,56},{16,0},{24,8},{32,16},{40,24},{48,32},{56,40},{64,11... | collective-permute-start | bytes 2211848 | tf_op jit(solution)/shard_map/ppermute | solution.py:88
  43.8 2.7 %collective-permute-start.18 = (bf16[48,4608]{1,0:T(8,128)(2,1)S(1)}, bf16[48,4608]{1,0:T(8,128)(2,1)S(1)}, u32[]{:S(2)}, u32[]{:S(2)}) collective-permute-start(bf16[48,4608]{1,0:T(8,128)(2,1)S(1)} %get-tuple-element.23), channel_id=1, source_target_pairs={{0,192},{8,200},{16,208},{24,216},{32,224},{40,232},{48,240},{56,2... | collective-permute-start | bytes 1327112 | tf_op jit(solution)/shard_map/ppermute | solution.py:88
  46.6 3.7 %shard_map.48 = f32[2,16,1024]{2,1,0:T(8,128)S(1)} custom-call(bf16[1024,4096]{1,0:T(8,128)(2,1)S(1)} %bitcast.35, bf16[1024,512]{1,0:T(8,128)(2,1)S(1)} %bitcast.41, bf16[64,4608]{1,0:T(8,128)(2,1)S(1)} %collective-permute-done.13.refs_0_, bf16[64,4608]{1,0:T(8,128)(2,1)S(1)} %collective-permute-done.14.refs_1_), custom_call_target="tpu_custom_call" | custom-call | flops 1207959552 | bytes 1179648 | tf_op jit(solution)/shard_map/pallas_call | solution.py:138
  50.5 4.7 %collective-permute-done.17.refs_2_ = bf16[48,4608]{1,0:T(8,128)(2,1)S(1)} collective-permute-done((bf16[48,4608]{1,0:T(8,128)(2,1)S(1)}, bf16[48,4608]{1,0:T(8,128)(2,1)S(1)}, u32[]{:S(2)}, u32[]{:S(2)}) %collective-permute-start.17) | collective-permute-done | bytes 442400 | tf_op jit(solution)/shard_map/ppermute | solution.py:88
  55.4 2.7 %collective-permute-start.28 = (bf16[32,4608]{1,0:T(8,128)(2,1)S(1)}, bf16[32,4608]{1,0:T(8,128)(2,1)S(1)}, u32[]{:S(2)}, u32[]{:S(2)}) collective-permute-start(bf16[32,4608]{1,0:T(8,128)(2,1)S(1)} %pad_maximum_fusion.16), channel_id=1, source_target_pairs={{0,48},{8,56},{16,0},{24,8},{32,16},{40,24},{48,32},{56,40},{64,11... | collective-permute-start | bytes 884744 | tf_op jit(solution)/shard_map/ppermute | solution.py:88
  58.1 2.1 %collective-permute-done.15.refs_0_ = bf16[80,4608]{1,0:T(8,128)(2,1)S(1)} collective-permute-done((bf16[80,4608]{1,0:T(8,128)(2,1)S(1)}, bf16[80,4608]{1,0:T(8,128)(2,1)S(1)}, u32[]{:S(2)}, u32[]{:S(2)}) %collective-permute-start.15) | collective-permute-done | bytes 737312 | tf_op jit(solution)/shard_map/ppermute | solution.py:88
  60.2 3.2 %collective-permute-done.27.refs_4_ = bf16[32,4608]{1,0:T(8,128)(2,1)S(1)} collective-permute-done((bf16[32,4608]{1,0:T(8,128)(2,1)S(1)}, bf16[32,4608]{1,0:T(8,128)(2,1)S(1)}, u32[]{:S(2)}, u32[]{:S(2)}) %collective-permute-start.27) | collective-permute-done | bytes 294944 | tf_op jit(solution)/shard_map/ppermute | solution.py:88
  63.5 2.0 %collective-permute-start.30 = (bf16[16,4608]{1,0:T(8,128)(2,1)S(1)}, bf16[16,4608]{1,0:T(8,128)(2,1)S(1)}, u32[]{:S(2)}, u32[]{:S(2)}) collective-permute-start(bf16[16,4608]{1,0:T(8,128)(2,1)S(1)} %get-tuple-element.16), channel_id=1, source_target_pairs={{0,192},{8,200},{16,208},{24,216},{32,224},{40,232},{48,240},{56,2... | collective-permute-start | bytes 442376 | tf_op jit(solution)/shard_map/ppermute | solution.py:88
  65.6 2.7 %collective-permute-start.32 = (bf16[16,4608]{1,0:T(8,128)(2,1)S(1)}, bf16[16,4608]{1,0:T(8,128)(2,1)S(1)}, u32[]{:S(2)}, u32[]{:S(2)}) collective-permute-start(bf16[16,4608]{1,0:T(8,128)(2,1)S(1)} %slice.192), channel_id=1, source_target_pairs={{0,48},{8,56},{16,0},{24,8},{32,16},{40,24},{48,32},{56,40},{64,11... | collective-permute-start | bytes 442376 | tf_op jit(solution)/shard_map/ppermute | solution.py:88
  68.4 3.4 %shard_map.49 = f32[2,32,1024]{2,1,0:T(8,128)S(1)} custom-call(bf16[1024,4096]{1,0:T(8,128)(2,1)S(1)} %bitcast.36, bf16[1024,512]{1,0:T(8,128)(2,1)S(1)} %bitcast.42, bf16[80,4608]{1,0:T(8,128)(2,1)S(1)} %collective-permute-done.15.refs_0_, bf16[80,4608]{1,0:T(8,128)(2,1)S(1)} %collective-permute-done.16.refs_1_, ...), custom_call_target="tpu_custom_call" | custom-call | flops 2415919104 | bytes 2359296 | tf_op jit(solution)/shard_map/pallas_call | solution.py:138
  72.0 4.2 %collective-permute-start.19 = (f32[48,1024]{1,0:T(8,128)S(1)}, f32[48,1024]{1,0:T(8,128)S(1)}, u32[]{:S(2)}, u32[]{:S(2)}) collective-permute-start(f32[48,1024]{1,0:T(8,128)S(1)} %pad_maximum_fusion.18), channel_id=1, source_target_pairs={{0,1},{1,0},{2,3},{3,2},{4,5},{5,4},{6,7},{7,6},{8,9},{9,8},{10,11... | collective-permute-start | bytes 589832 | tf_op jit(solution)/shard_map/ppermute | solution.py:157
  76.2 2.7 %collective-permute-start.24 = (bf16[32,4608]{1,0:T(8,128)(2,1)S(1)}, bf16[32,4608]{1,0:T(8,128)(2,1)S(1)}, u32[]{:S(2)}, u32[]{:S(2)}) collective-permute-start(bf16[32,4608]{1,0:T(8,128)(2,1)S(1)} %pad_maximum_fusion.13), channel_id=1, source_target_pairs={{0,48},{8,56},{16,0},{24,8},{32,16},{40,24},{48,32},{56,40},{64,11... | collective-permute-start | bytes 884744 | tf_op jit(solution)/shard_map/ppermute | solution.py:88
  78.9 3.4 %shard_map.51 = f32[2,8,1024]{2,1,0:T(8,128)S(1)} custom-call(bf16[1024,4096]{1,0:T(8,128)(2,1)S(1)} %bitcast.37, bf16[1024,512]{1,0:T(8,128)(2,1)S(1)} %bitcast.43, bf16[16,4608]{1,0:T(8,128)(2,1)S(1)} %collective-permute-done.29.refs_0_, bf16[16,4608]{1,0:T(8,128)(2,1)S(1)} %collective-permute-done.30.refs_1_, ...), custom_call_target="tpu_custom_call" | custom-call | flops 603979776 | bytes 589824 | tf_op jit(solution)/shard_map/pallas_call | solution.py:138
  82.4 6.3 %collective-permute-start.10 = (f32[48,1024]{1,0:T(8,128)S(1)}, f32[48,1024]{1,0:T(8,128)S(1)}, u32[]{:S(2)}, u32[]{:S(2)}) collective-permute-start(f32[48,1024]{1,0:T(8,128)S(1)} %maximum_add_fusion), channel_id=1, source_target_pairs={{0,2},{1,7},{2,0},{3,5},{4,6},{5,3},{6,4},{7,1},{8,10},{9,15},{10,... | collective-permute-start | bytes 589832 | tf_op jit(solution)/shard_map/ppermute | solution.py:158
  88.8 3.8 %shard_map.50 = f32[2,24,1024]{2,1,0:T(8,128)S(1)} custom-call(bf16[1024,4096]{1,0:T(8,128)(2,1)S(1)} %bitcast.38, bf16[1024,512]{1,0:T(8,128)(2,1)S(1)} %bitcast.44, bf16[32,4608]{1,0:T(8,128)(2,1)S(1)} %collective-permute-done.23.refs_0_, bf16[32,4608]{1,0:T(8,128)(2,1)S(1)} %collective-permute-done.24.refs_1_, ...), custom_call_target="tpu_custom_call" | custom-call | flops 1811939328 | bytes 1769472 | tf_op jit(solution)/shard_map/pallas_call | solution.py:138
  95.3 2.2 %collective-permute-done.20 = f32[48,1024]{1,0:T(8,128)S(1)} collective-permute-done((f32[48,1024]{1,0:T(8,128)S(1)}, f32[48,1024]{1,0:T(8,128)S(1)}, u32[]{:S(2)}, u32[]{:S(2)}) %collective-permute-start.20) | collective-permute-done | bytes 196640 | tf_op jit(solution)/shard_map/ppermute | solution.py:158
  97.5 4.2 %collective-permute-start.34 = (f32[32,1024]{1,0:T(8,128)S(1)}, f32[32,1024]{1,0:T(8,128)S(1)}, u32[]{:S(2)}, u32[]{:S(2)}) collective-permute-start(f32[32,1024]{1,0:T(8,128)S(1)} %maximum_add_fusion.2), channel_id=1, source_target_pairs={{0,2},{1,7},{2,0},{3,5},{4,6},{5,3},{6,4},{7,1},{8,10},{9,15},{10,... | collective-permute-start | bytes 393224 | tf_op jit(solution)/shard_map/ppermute | solution.py:158
  101.8 2.5 %collective-permute-start.21 = (f32[48,1024]{1,0:T(8,128)S(1)}, f32[48,1024]{1,0:T(8,128)S(1)}, u32[]{:S(2)}, u32[]{:S(2)}) collective-permute-start(f32[48,1024]{1,0:T(8,128)S(1)} %add.31), channel_id=1, source_target_pairs={{0,6},{1,3},{2,4},{3,1},{4,2},{5,7},{6,0},{7,5},{8,14},{9,11},{10,... | collective-permute-start | bytes 589832 | tf_op jit(solution)/shard_map/ppermute | solution.py:159
  104.3 3.9 %collective-permute-done.34 = f32[32,1024]{1,0:T(8,128)S(1)} collective-permute-done((f32[32,1024]{1,0:T(8,128)S(1)}, f32[32,1024]{1,0:T(8,128)S(1)}, u32[]{:S(2)}, u32[]{:S(2)}) %collective-permute-start.34) | collective-permute-done | bytes 131104 | tf_op jit(solution)/shard_map/ppermute | solution.py:158
  108.2 4.9 %collective-permute-start.35 = (f32[32,1024]{1,0:T(8,128)S(1)}, f32[32,1024]{1,0:T(8,128)S(1)}, u32[]{:S(2)}, u32[]{:S(2)}) collective-permute-start(f32[32,1024]{1,0:T(8,128)S(1)} %add.34), channel_id=1, source_target_pairs={{0,6},{1,3},{2,4},{3,1},{4,2},{5,7},{6,0},{7,5},{8,14},{9,11},{10,... | collective-permute-start | bytes 393224 | tf_op jit(solution)/shard_map/ppermute | solution.py:159
  113.9 2.6 %collective-permute-done.35 = f32[32,1024]{1,0:T(8,128)S(1)} collective-permute-done((f32[32,1024]{1,0:T(8,128)S(1)}, f32[32,1024]{1,0:T(8,128)S(1)}, u32[]{:S(2)}, u32[]{:S(2)}) %collective-permute-start.35) | collective-permute-done | bytes 131104 | tf_op jit(solution)/shard_map/ppermute | solution.py:159
  (105 shorter events, 12.9 us)
Async XLA Ops:
  1.2 9.3 %collective-permute-start.4 = (bf16[32,4608]{1,0:T(8,128)(2,1)S(1)}, bf16[32,4608]{1,0:T(8,128)(2,1)S(1)}, u32[]{:S(2)}, u32[]{:S(2)}) collective-permute-start(bf16[32,4608]{1,0:T(8,128)(2,1)S(1)} %bitcast.45), channel_id=1, source_target_pairs={{0,192},{8,200},{16,208},{24,216},{32,224},{40,232},{48,240},{56,2... | collective-permute-start | bytes 884744 | tf_op jit(solution)/shard_map/ppermute | solution.py:88
  7.3 8.5 %collective-permute-start.3 = (bf16[32,4608]{1,0:T(8,128)(2,1)S(1)}, bf16[32,4608]{1,0:T(8,128)(2,1)S(1)}, u32[]{:S(2)}, u32[]{:S(2)}) collective-permute-start(bf16[32,4608]{1,0:T(8,128)(2,1)S(1)} %bitcast.47), channel_id=1, source_target_pairs={{0,64},{8,72},{16,80},{24,88},{32,96},{40,104},{48,112},{56,120},{... | collective-permute-start | bytes 884744 | tf_op jit(solution)/shard_map/ppermute | solution.py:88
  7.3 8.5 %collective-permute-start.1 = (bf16[32,4608]{1,0:T(8,128)(2,1)S(1)}, bf16[32,4608]{1,0:T(8,128)(2,1)S(1)}, u32[]{:S(2)}, u32[]{:S(2)}) collective-permute-start(bf16[32,4608]{1,0:T(8,128)(2,1)S(1)} %bitcast.48), channel_id=1, source_target_pairs={{0,16},{8,24},{16,32},{24,40},{32,48},{40,56},{48,0},{56,8},{64,80... | collective-permute-start | bytes 884744 | tf_op jit(solution)/shard_map/ppermute | solution.py:88
  7.3 8.5 %collective-permute-start = (bf16[32,4608]{1,0:T(8,128)(2,1)S(1)}, bf16[32,4608]{1,0:T(8,128)(2,1)S(1)}, u32[]{:S(2)}, u32[]{:S(2)}) collective-permute-start(bf16[32,4608]{1,0:T(8,128)(2,1)S(1)} %bitcast.49), channel_id=1, source_target_pairs={{0,8},{8,0},{16,24},{24,16},{32,40},{40,32},{48,56},{56,48},{64,72... | collective-permute-start | bytes 884744 | tf_op jit(solution)/shard_map/ppermute | solution.py:88
  16.0 12.9 %collective-permute-start.5 = (bf16[48,4608]{1,0:T(8,128)(2,1)S(1)}, bf16[48,4608]{1,0:T(8,128)(2,1)S(1)}, u32[]{:S(2)}, u32[]{:S(2)}) collective-permute-start(bf16[48,4608]{1,0:T(8,128)(2,1)S(1)} %get-tuple-element.28), channel_id=1, source_target_pairs={{0,16},{8,24},{16,32},{24,40},{32,48},{40,56},{48,0},{56,8},{64,80... | collective-permute-start | bytes 1327112 | tf_op jit(solution)/shard_map/ppermute | solution.py:88
  16.1 15.5 %collective-permute-start.6 = (bf16[48,4608]{1,0:T(8,128)(2,1)S(1)}, bf16[48,4608]{1,0:T(8,128)(2,1)S(1)}, u32[]{:S(2)}, u32[]{:S(2)}) collective-permute-start(bf16[48,4608]{1,0:T(8,128)(2,1)S(1)} %get-tuple-element.26), channel_id=1, source_target_pairs={{0,48},{8,56},{16,0},{24,8},{32,16},{40,24},{48,32},{56,40},{64,11... | collective-permute-start | bytes 1327112 | tf_op jit(solution)/shard_map/ppermute | solution.py:88
  18.7 12.8 %collective-permute-start.7 = (bf16[48,4608]{1,0:T(8,128)(2,1)S(1)}, bf16[48,4608]{1,0:T(8,128)(2,1)S(1)}, u32[]{:S(2)}, u32[]{:S(2)}) collective-permute-start(bf16[48,4608]{1,0:T(8,128)(2,1)S(1)} %get-tuple-element.27), channel_id=1, source_target_pairs={{0,64},{8,72},{16,80},{24,88},{32,96},{40,104},{48,112},{56,120},{... | collective-permute-start | bytes 1327112 | tf_op jit(solution)/shard_map/ppermute | solution.py:88
  18.7 12.8 %collective-permute-start.8 = (bf16[48,4608]{1,0:T(8,128)(2,1)S(1)}, bf16[48,4608]{1,0:T(8,128)(2,1)S(1)}, u32[]{:S(2)}, u32[]{:S(2)}) collective-permute-start(bf16[48,4608]{1,0:T(8,128)(2,1)S(1)} %get-tuple-element.25), channel_id=1, source_target_pairs={{0,192},{8,200},{16,208},{24,216},{32,224},{40,232},{48,240},{56,2... | collective-permute-start | bytes 1327112 | tf_op jit(solution)/shard_map/ppermute | solution.py:88
  21.4 22.2 %collective-permute-start.13 = (bf16[64,4608]{1,0:T(8,128)(2,1)S(1)}, bf16[64,4608]{1,0:T(8,128)(2,1)S(1)}, u32[]{:S(2)}, u32[]{:S(2)}) collective-permute-start(bf16[64,4608]{1,0:T(8,128)(2,1)S(1)} %constant_dynamic-update-slice_fusion), channel_id=1, source_target_pairs={{0,64},{8,72},{16,80},{24,88},{32,96},{40,104},{48,112},{56,120},{... | collective-permute-start | bytes 1769480 | tf_op jit(solution)/shard_map/ppermute | solution.py:88
  28.8 15.0 %collective-permute-start.14 = (bf16[64,4608]{1,0:T(8,128)(2,1)S(1)}, bf16[64,4608]{1,0:T(8,128)(2,1)S(1)}, u32[]{:S(2)}, u32[]{:S(2)}) collective-permute-start(bf16[64,4608]{1,0:T(8,128)(2,1)S(1)} %constant_dynamic-update-slice_fusion), channel_id=1, source_target_pairs={{0,192},{8,200},{16,208},{24,216},{32,224},{40,232},{48,240},{56,2... | collective-permute-start | bytes 1769480 | tf_op jit(solution)/shard_map/ppermute | solution.py:88
  35.5 14.8 %collective-permute-start.9 = (f32[48,1024]{1,0:T(8,128)S(1)}, f32[48,1024]{1,0:T(8,128)S(1)}, u32[]{:S(2)}, u32[]{:S(2)}) collective-permute-start(f32[48,1024]{1,0:T(8,128)S(1)} %pad_maximum_fusion.17), channel_id=1, source_target_pairs={{0,1},{1,0},{2,3},{3,2},{4,5},{5,4},{6,7},{7,6},{8,9},{9,8},{10,11... | collective-permute-start | bytes 589832 | tf_op jit(solution)/shard_map/ppermute | solution.py:157
  40.8 19.4 %collective-permute-start.15 = (bf16[80,4608]{1,0:T(8,128)(2,1)S(1)}, bf16[80,4608]{1,0:T(8,128)(2,1)S(1)}, u32[]{:S(2)}, u32[]{:S(2)}) collective-permute-start(bf16[80,4608]{1,0:T(8,128)(2,1)S(1)} %get-tuple-element.14), channel_id=1, source_target_pairs={{0,16},{8,24},{16,32},{24,40},{32,48},{40,56},{48,0},{56,8},{64,80... | collective-permute-start | bytes 2211848 | tf_op jit(solution)/shard_map/ppermute | solution.py:88
  40.9 24.7 %collective-permute-start.16 = (bf16[80,4608]{1,0:T(8,128)(2,1)S(1)}, bf16[80,4608]{1,0:T(8,128)(2,1)S(1)}, u32[]{:S(2)}, u32[]{:S(2)}) collective-permute-start(bf16[80,4608]{1,0:T(8,128)(2,1)S(1)} %get-tuple-element.13), channel_id=1, source_target_pairs={{0,48},{8,56},{16,0},{24,8},{32,16},{40,24},{48,32},{56,40},{64,11... | collective-permute-start | bytes 2211848 | tf_op jit(solution)/shard_map/ppermute | solution.py:88
  43.7 11.5 %collective-permute-start.17 = (bf16[48,4608]{1,0:T(8,128)(2,1)S(1)}, bf16[48,4608]{1,0:T(8,128)(2,1)S(1)}, u32[]{:S(2)}, u32[]{:S(2)}) collective-permute-start(bf16[48,4608]{1,0:T(8,128)(2,1)S(1)} %get-tuple-element.24), channel_id=1, source_target_pairs={{0,64},{8,72},{16,80},{24,88},{32,96},{40,104},{48,112},{56,120},{... | collective-permute-start | bytes 1327112 | tf_op jit(solution)/shard_map/ppermute | solution.py:88
  43.8 11.4 %collective-permute-start.18 = (bf16[48,4608]{1,0:T(8,128)(2,1)S(1)}, bf16[48,4608]{1,0:T(8,128)(2,1)S(1)}, u32[]{:S(2)}, u32[]{:S(2)}) collective-permute-start(bf16[48,4608]{1,0:T(8,128)(2,1)S(1)} %get-tuple-element.23), channel_id=1, source_target_pairs={{0,192},{8,200},{16,208},{24,216},{32,224},{40,232},{48,240},{56,2... | collective-permute-start | bytes 1327112 | tf_op jit(solution)/shard_map/ppermute | solution.py:88
  50.3 38.4 %collective-permute-start.25 = (bf16[32,4608]{1,0:T(8,128)(2,1)S(1)}, bf16[32,4608]{1,0:T(8,128)(2,1)S(1)}, u32[]{:S(2)}, u32[]{:S(2)}) collective-permute-start(bf16[32,4608]{1,0:T(8,128)(2,1)S(1)} %pad_maximum_fusion.14), channel_id=1, source_target_pairs={{0,64},{8,72},{16,80},{24,88},{32,96},{40,104},{48,112},{56,120},{... | collective-permute-start | bytes 884744 | tf_op jit(solution)/shard_map/ppermute | solution.py:88
  55.3 8.2 %collective-permute-start.27 = (bf16[32,4608]{1,0:T(8,128)(2,1)S(1)}, bf16[32,4608]{1,0:T(8,128)(2,1)S(1)}, u32[]{:S(2)}, u32[]{:S(2)}) collective-permute-start(bf16[32,4608]{1,0:T(8,128)(2,1)S(1)} %pad_maximum_fusion.16), channel_id=1, source_target_pairs={{0,16},{8,24},{16,32},{24,40},{32,48},{40,56},{48,0},{56,8},{64,80... | collective-permute-start | bytes 884744 | tf_op jit(solution)/shard_map/ppermute | solution.py:88
  55.4 10.1 %collective-permute-start.28 = (bf16[32,4608]{1,0:T(8,128)(2,1)S(1)}, bf16[32,4608]{1,0:T(8,128)(2,1)S(1)}, u32[]{:S(2)}, u32[]{:S(2)}) collective-permute-start(bf16[32,4608]{1,0:T(8,128)(2,1)S(1)} %pad_maximum_fusion.16), channel_id=1, source_target_pairs={{0,48},{8,56},{16,0},{24,8},{32,16},{40,24},{48,32},{56,40},{64,11... | collective-permute-start | bytes 884744 | tf_op jit(solution)/shard_map/ppermute | solution.py:88
  60.2 11.7 %collective-permute-start.29 = (bf16[16,4608]{1,0:T(8,128)(2,1)S(1)}, bf16[16,4608]{1,0:T(8,128)(2,1)S(1)}, u32[]{:S(2)}, u32[]{:S(2)}) collective-permute-start(bf16[16,4608]{1,0:T(8,128)(2,1)S(1)} %get-tuple-element.18), channel_id=1, source_target_pairs={{0,64},{8,72},{16,80},{24,88},{32,96},{40,104},{48,112},{56,120},{... | collective-permute-start | bytes 442376 | tf_op jit(solution)/shard_map/ppermute | solution.py:88
  63.5 8.5 %collective-permute-start.30 = (bf16[16,4608]{1,0:T(8,128)(2,1)S(1)}, bf16[16,4608]{1,0:T(8,128)(2,1)S(1)}, u32[]{:S(2)}, u32[]{:S(2)}) collective-permute-start(bf16[16,4608]{1,0:T(8,128)(2,1)S(1)} %get-tuple-element.16), channel_id=1, source_target_pairs={{0,192},{8,200},{16,208},{24,216},{32,224},{40,232},{48,240},{56,2... | collective-permute-start | bytes 442376 | tf_op jit(solution)/shard_map/ppermute | solution.py:88
  65.5 10.8 %collective-permute-start.31 = (bf16[16,4608]{1,0:T(8,128)(2,1)S(1)}, bf16[16,4608]{1,0:T(8,128)(2,1)S(1)}, u32[]{:S(2)}, u32[]{:S(2)}) collective-permute-start(bf16[16,4608]{1,0:T(8,128)(2,1)S(1)} %slice.191), channel_id=1, source_target_pairs={{0,16},{8,24},{16,32},{24,40},{32,48},{40,56},{48,0},{56,8},{64,80... | collective-permute-start | bytes 442376 | tf_op jit(solution)/shard_map/ppermute | solution.py:88
  65.6 10.6 %collective-permute-start.32 = (bf16[16,4608]{1,0:T(8,128)(2,1)S(1)}, bf16[16,4608]{1,0:T(8,128)(2,1)S(1)}, u32[]{:S(2)}, u32[]{:S(2)}) collective-permute-start(bf16[16,4608]{1,0:T(8,128)(2,1)S(1)} %slice.192), channel_id=1, source_target_pairs={{0,48},{8,56},{16,0},{24,8},{32,16},{40,24},{48,32},{56,40},{64,11... | collective-permute-start | bytes 442376 | tf_op jit(solution)/shard_map/ppermute | solution.py:88
  71.9 16.9 %collective-permute-start.26 = (bf16[32,4608]{1,0:T(8,128)(2,1)S(1)}, bf16[32,4608]{1,0:T(8,128)(2,1)S(1)}, u32[]{:S(2)}, u32[]{:S(2)}) collective-permute-start(bf16[32,4608]{1,0:T(8,128)(2,1)S(1)} %pad_maximum_fusion.15), channel_id=1, source_target_pairs={{0,192},{8,200},{16,208},{24,216},{32,224},{40,232},{48,240},{56,2... | collective-permute-start | bytes 884744 | tf_op jit(solution)/shard_map/ppermute | solution.py:88
  72.0 10.3 %collective-permute-start.19 = (f32[48,1024]{1,0:T(8,128)S(1)}, f32[48,1024]{1,0:T(8,128)S(1)}, u32[]{:S(2)}, u32[]{:S(2)}) collective-permute-start(f32[48,1024]{1,0:T(8,128)S(1)} %pad_maximum_fusion.18), channel_id=1, source_target_pairs={{0,1},{1,0},{2,3},{3,2},{4,5},{5,4},{6,7},{7,6},{8,9},{9,8},{10,11... | collective-permute-start | bytes 589832 | tf_op jit(solution)/shard_map/ppermute | solution.py:157
  76.2 12.6 %collective-permute-start.23 = (bf16[32,4608]{1,0:T(8,128)(2,1)S(1)}, bf16[32,4608]{1,0:T(8,128)(2,1)S(1)}, u32[]{:S(2)}, u32[]{:S(2)}) collective-permute-start(bf16[32,4608]{1,0:T(8,128)(2,1)S(1)} %pad_maximum_fusion.12), channel_id=1, source_target_pairs={{0,16},{8,24},{16,32},{24,40},{32,48},{40,56},{48,0},{56,8},{64,80... | collective-permute-start | bytes 884744 | tf_op jit(solution)/shard_map/ppermute | solution.py:88
  76.2 12.6 %collective-permute-start.24 = (bf16[32,4608]{1,0:T(8,128)(2,1)S(1)}, bf16[32,4608]{1,0:T(8,128)(2,1)S(1)}, u32[]{:S(2)}, u32[]{:S(2)}) collective-permute-start(bf16[32,4608]{1,0:T(8,128)(2,1)S(1)} %pad_maximum_fusion.13), channel_id=1, source_target_pairs={{0,48},{8,56},{16,0},{24,8},{32,16},{40,24},{48,32},{56,40},{64,11... | collective-permute-start | bytes 884744 | tf_op jit(solution)/shard_map/ppermute | solution.py:88
  82.4 11.4 %collective-permute-start.10 = (f32[48,1024]{1,0:T(8,128)S(1)}, f32[48,1024]{1,0:T(8,128)S(1)}, u32[]{:S(2)}, u32[]{:S(2)}) collective-permute-start(f32[48,1024]{1,0:T(8,128)S(1)} %maximum_add_fusion), channel_id=1, source_target_pairs={{0,2},{1,7},{2,0},{3,5},{4,6},{5,3},{6,4},{7,1},{8,10},{9,15},{10,... | collective-permute-start | bytes 589832 | tf_op jit(solution)/shard_map/ppermute | solution.py:158
  88.7 8.8 %collective-permute-start.20 = (f32[48,1024]{1,0:T(8,128)S(1)}, f32[48,1024]{1,0:T(8,128)S(1)}, u32[]{:S(2)}, u32[]{:S(2)}) collective-permute-start(f32[48,1024]{1,0:T(8,128)S(1)} %maximum_add_fusion.1), channel_id=1, source_target_pairs={{0,2},{1,7},{2,0},{3,5},{4,6},{5,3},{6,4},{7,1},{8,10},{9,15},{10,... | collective-permute-start | bytes 589832 | tf_op jit(solution)/shard_map/ppermute | solution.py:158
  93.8 19.4 %collective-permute-start.11 = (f32[48,1024]{1,0:T(8,128)S(1)}, f32[48,1024]{1,0:T(8,128)S(1)}, u32[]{:S(2)}, u32[]{:S(2)}) collective-permute-start(f32[48,1024]{1,0:T(8,128)S(1)} %add.28), channel_id=1, source_target_pairs={{0,6},{1,3},{2,4},{3,1},{4,2},{5,7},{6,0},{7,5},{8,14},{9,11},{10,... | collective-permute-start | bytes 589832 | tf_op jit(solution)/shard_map/ppermute | solution.py:159
  97.5 10.7 %collective-permute-start.34 = (f32[32,1024]{1,0:T(8,128)S(1)}, f32[32,1024]{1,0:T(8,128)S(1)}, u32[]{:S(2)}, u32[]{:S(2)}) collective-permute-start(f32[32,1024]{1,0:T(8,128)S(1)} %maximum_add_fusion.2), channel_id=1, source_target_pairs={{0,2},{1,7},{2,0},{3,5},{4,6},{5,3},{6,4},{7,1},{8,10},{9,15},{10,... | collective-permute-start | bytes 393224 | tf_op jit(solution)/shard_map/ppermute | solution.py:158
  101.8 11.5 %collective-permute-start.21 = (f32[48,1024]{1,0:T(8,128)S(1)}, f32[48,1024]{1,0:T(8,128)S(1)}, u32[]{:S(2)}, u32[]{:S(2)}) collective-permute-start(f32[48,1024]{1,0:T(8,128)S(1)} %add.31), channel_id=1, source_target_pairs={{0,6},{1,3},{2,4},{3,1},{4,2},{5,7},{6,0},{7,5},{8,14},{9,11},{10,... | collective-permute-start | bytes 589832 | tf_op jit(solution)/shard_map/ppermute | solution.py:159
  108.2 8.2 %collective-permute-start.35 = (f32[32,1024]{1,0:T(8,128)S(1)}, f32[32,1024]{1,0:T(8,128)S(1)}, u32[]{:S(2)}, u32[]{:S(2)}) collective-permute-start(f32[32,1024]{1,0:T(8,128)S(1)} %add.34), channel_id=1, source_target_pairs={{0,6},{1,3},{2,4},{3,1},{4,2},{5,7},{6,0},{7,5},{8,14},{9,11},{10,... | collective-permute-start | bytes 393224 | tf_op jit(solution)/shard_map/ppermute | solution.py:159
  (10 other events, 41.9 us)

commit v2 on v1

--- a/solution.py
+++ b/solution.py
@@ -82,9 +82,13 @@
             return lax.slice_in_dim(buf, at, at + HALF, axis=0)
         return jnp.concatenate([self.get(piece[:3] + (h,)) for h in (0, 1)], axis=0)
 
-    def send(self, step, pieces):
+    def pack(self, pieces, *behind):
         parts = [self.get(p) for p in pieces]
         data = parts[0] if len(parts) == 1 else jnp.concatenate(parts, axis=0)
+        return (after(data, *behind) if behind else data), pieces
+
+    def send(self, step, packed):
+        data, pieces = packed
         got = lax.ppermute(data, "dp", STEPS[step])
         at, names = 0, []
         for p in pieces:
@@ -95,13 +99,18 @@
         return got, names
 
 
-def term_kernel(n_buf, plan, blocks, x_ref, g_ref, *refs):
-    bufs, out_ref, fac = refs[:n_buf], refs[n_buf], refs[n_buf + 1]
+def after(value, *others):
+    return lax.optimization_barrier((value,) + others)[0]
+
+
+def term_kernel(segments, plan, blocks, x_ref, g_ref, *refs):
+    bufs, out_ref, fac = refs[: len(segments)], refs[-2], refs[-1]
     core = lax.rem(lax.axis_index("layer"), 2)
     at = 0
-    for b in bufs:
-        fac[at : at + b.shape[0], :] = b[...]
-        at += b.shape[0]
+    for b, parts in zip(bufs, segments):
+        for begin, n in parts:
+            fac[at : at + n, :] = b[begin : begin + n, :]
+            at += n
     depth = x_ref.shape[1]
     half = len(blocks) // 2
 
@@ -124,40 +133,41 @@
             out_ref[which, row * QPD : (row + 1) * QPD, pl.ds(t, TB)] = total
 
 
-def term(x, g, received):
-    plan, at = {}, 0
+def term(x, g, received, leave=()):
+    plan, segments, at = {}, [], 0
     for _, names in received:
+        parts, row = [], 0
         for name in names:
             n = piece_rows(name)
-            plan.setdefault(name[:3], []).extend(range(at, at + n, QPD))
-            at += n
+            if name[:3] not in leave:
+                parts.append((row, n))
+                plan.setdefault(name[:3], []).extend(range(at, at + n, QPD))
+                at += n
+            row += n
+        segments.append(parts)
     blocks = sorted(plan)
     assert all(len(v) == RANK for v in plan.values()) and len(blocks) % 2 == 0
     vmem = pl.BlockSpec(memory_space=pltpu.VMEM)
     tokens, width = x.shape[0], x.shape[1] + g.shape[1]
     out = pl.pallas_call(
-        functools.partial(term_kernel, len(received), plan, blocks),
+        functools.partial(term_kernel, segments, plan, blocks),
         out_shape=jax.ShapeDtypeStruct((2, len(blocks) // 2 * QPD, tokens), jnp.float32),
         in_specs=[vmem] * (2 + len(received)),
         out_specs=vmem,
         scratch_shapes=[pltpu.VMEM((at, width), jnp.bfloat16)],
         compiler_params=pltpu.CompilerParams(vmem_limit_bytes=20 * 2**20),
-        cost_estimate=pl.CostEstimate(
-            flops=2 * at * width * tokens, bytes_accessed=at * width * 2, transcendentals=0
-        ),
+        cost_estimate=pl.CostEstimate(flops=1 * 2 * at * width * tokens, bytes_accessed=1, transcendentals=0),
     )(x, g, *[b for b, _ in received])
     return out, blocks
 
 
-def layer_sum(terms):
-    keep = [t[0] for t in terms]
-    send = [t[1] for t in terms]
-    keep = keep[0] if len(keep) == 1 else jnp.concatenate(keep, axis=0)
-    send = send[0] if len(send) == 1 else jnp.concatenate(send, axis=0)
-    mine = keep + lax.ppermute(send, "layer", CORE_SWAP)
-    mine = mine + lax.ppermute(mine, "layer", PAIR_A)
-    mine = mine + lax.ppermute(mine, "layer", PAIR_B)
-    return mine, lax.ppermute(mine, "layer", CORE_SWAP)
+def to_core(terms, h):
+    parts = [t[h] for t in terms]
+    return parts[0] if len(parts) == 1 else jnp.concatenate(parts, axis=0)
+
+
+def layer_move(value, pairs):
+    return lax.ppermute(value, "layer", pairs)
 
 
 def place_kernel(groups, *refs):
@@ -194,52 +204,80 @@
 
 
 def shards(layer_inputs, output_grads, input_factors, output_factors):
-    x, g = layer_inputs[0], output_grads[0]
+    acts, grads = layer_inputs[0], output_grads[0]
     own = jnp.concatenate([input_factors[:, 0], output_factors[:, 0]], axis=2)
     own = jnp.swapaxes(own, 0, 1).reshape(ROWS, own.shape[2])
     have = Pieces(own)
     A, B = 0, 1
-    rz = have.send("Z", [(A, 0, 0, None)])
-    first = [have.send(s, [(A, 0, 0, None)]) for s in ("XP", "XM", "YP", "YM")]
-    c0 = [(own, [(A, 0, 0, None)]), rz] + first
-    c1 = [
-        have.send("XP", [(A, -1, 0, 1), (B, 0, 0, None)]),
-        have.send("XM", [(A, 1, 0, 0), (B, 0, 0, None)]),
-        have.send("YP", [(A, 0, -1, 1), (B, 0, 0, None)]),
-        have.send("YM", [(A, 0, 1, 0), (B, 0, 0, None)]),
-    ]
-    c2 = [have.send(s, [(A, 1, 0, None), (A, -1, 0, None)]) for s in ("YP", "YM")]
-    c3 = [
-        have.send("XP", [(B, -1, 0, 1), (B, 0, 1, None), (B, 0, -1, None)]),
-        have.send("XM", [(B, 1, 0, 0), (B, 0, 1, None), (B, 0, -1, None)]),
-        have.send("YP", [(B, 0, -1, 1), (A, 2, 0, None)]),
-        have.send("YM", [(B, 0, 1, 0), (A, 2, 0, None)]),
-    ]
-    c4 = [
-        have.send("XP", [(B, -1, 1, 1), (B, -1, -1, 1)]),
-        have.send("XM", [(B, 1, 1, 0), (B, 1, -1, 0)]),
-        have.send("YP", [(A, 1, -1, 1), (A, -1, -1, 1)]),
-        have.send("YM", [(A, 1, 1, 0), (A, -1, 1, 0)]),
-        have.send("XP", [(B, 0, 2, None)]),
-        have.send("XM", [(B, 0, 2, None)]),
-    ]
-    c5 = [
-        have.send("YP", [(A, 2, -1, 1)]),
-        have.send("YM", [(A, 2, 1, 0)]),
-        have.send("XP", [(B, -1, 2, 1)]),
-        have.send("XM", [(B, 1, 2, 0)]),
-    ]
-    groups, arrays = [], []
-    for chunks in ((c0, c1), (c2, c3), (c4, c5)):
-        terms, halves = [], ([], [])
-        for c in chunks:
-            out, blocks = term(x, g, c)
-            terms.append(out)
-            halves[0].extend(blocks[: len(blocks) // 2])
-            halves[1].extend(blocks[len(blocks) // 2 :])
-        arrays.extend(layer_sum(terms))
-        groups.append(halves)
-    return place(groups, arrays, lax.axis_size("dp") * QPD)
+    B0 = (B, 0, 0, None)
+    mine = (own, [(A, 0, 0, None)])
+    z0 = have.send("Z", mine)
+    xy0 = [have.send(s, mine) for s in ("XP", "XM", "YP", "YM")]
+
+    x = [have.pack([(A, -1, 0, 1), B0]), have.pack([(A, 1, 0, 0), B0])]
+    y = [have.pack([(A, 0, -1, 1), B0]), have.pack([(A, 0, 1, 0), B0])]
+    x1 = [have.send("XP", x[0]), have.send("XM", x[1])]
+    y1 = [have.send("YP", y[0]), have.send("YM", y[1])]
+
+    y = [have.pack([(B, 0, -1, 1), (A, 2, 0, None)]), have.pack([(B, 0, 1, 0), (A, 2, 0, None)])]
+    x = [
+        have.pack([(B, -1, 0, 1), (B, 0, 1, None), (B, 0, -1, None)]),
+        have.pack([(B, 1, 0, 0), (B, 0, 1, None), (B, 0, -1, None)]),
+    ]
+    y2 = [have.send("YP", y[0]), have.send("YM", y[1])]
+    x2 = [have.send("XP", x[0]), have.send("XM", x[1])]
+
+    t0, blocks0 = term(acts, grads, [(after(z0[0], x[0][0], x[1][0], y[0][0], y[1][0]), z0[1])] + xy0 + x1)
+
+    r0 = layer_move(to_core((t0,), 1), CORE_SWAP)
+
+    y = have.pack([(A, 1, 0, None), (A, -1, 0, None)], t0)
+    y3 = [have.send("YP", y), have.send("YM", y)]
+
+    x = [
+        have.pack([(B, 0, 2, None), (B, -1, 1, 1), (B, -1, -1, 1)], y3[0][0], y3[1][0]),
+        have.pack([(B, 0, 2, None), (B, 1, 1, 0), (B, 1, -1, 0)], y3[0][0], y3[1][0]),
+    ]
+    y = [
+        have.pack([(A, 1, -1, 1), (A, -1, -1, 1), (A, 2, -1, 1)], x2[0][0], x2[1][0]),
+        have.pack([(A, 1, 1, 0), (A, -1, 1, 0), (A, 2, 1, 0)], x2[0][0], x2[1][0]),
+    ]
+    x3 = [have.send("XP", x[0]), have.send("XM", x[1])]
+    y4 = [have.send("YP", y[0]), have.send("YM", y[1])]
+
+    s0 = to_core((t0,), 0) + after(r0, x[0][0], x[1][0], y[0][0], y[1][0])
+    r0 = layer_move(s0, PAIR_A)
+    late = {(B, i, j) for i in (-1, 1) for j in (-1, 1)}
+    t1, blocks1 = term(acts, grads, [(after(own, s0), mine[1])] + y1 + y2 + x2, late)
+    s0 = s0 + after(r0, t1)
+    r0 = layer_move(s0, PAIR_B)
+    t2, blocks2 = term(acts, grads, x2 + [(after(b, s0), n) for b, n in y3], {(B, 2, 0)})
+    r1 = layer_move(to_core((t1, t2), 1), CORE_SWAP)
+    s0 = s0 + after(r0, t2)
+
+    x = [have.pack([(B, -1, 2, 1)], t2), have.pack([(B, 1, 2, 0)], t2)]
+    x4 = [have.send("XP", x[0]), have.send("XM", x[1])]
+    s1 = to_core((t1, t2), 0) + after(r1, x[0][0], x[1][0])
+    r1 = layer_move(s1, PAIR_A)
+
+    t3, blocks3 = term(acts, grads, x3 + [(after(b, s1), n) for b, n in y4] + x4)
+    r2 = layer_move(to_core((t3,), 1), CORE_SWAP)
+    s1 = s1 + after(r1, t3)
+    r1 = layer_move(s1, PAIR_B)
+    s2 = to_core((t3,), 0) + after(r2, s1)
+    r2 = layer_move(s2, PAIR_A)
+    o0 = layer_move(s0, CORE_SWAP)
+    s1 = s1 + after(r1, s2)
+    o1 = layer_move(s1, CORE_SWAP)
+    s2 = s2 + after(r2, s1)
+    s2 = s2 + layer_move(s2, PAIR_B)
+    o2 = layer_move(s2, CORE_SWAP)
+
+    def halves(*blocks):
+        return [sum((b[: len(b) // 2] for b in blocks), []), sum((b[len(b) // 2 :] for b in blocks), [])]
+
+    groups = [halves(blocks0), halves(blocks1, blocks2), halves(blocks3)]
+    return place(groups, [s0, o0, s1, o1, s2, o2], lax.axis_size("dp") * QPD)
 
 
 def solution(mesh):

time: 119 us -> 114 us (0.958)
  Pallas kernels: 23.3 us -> 15 us
  waiting for transfers between devices: 27.9 us -> 36.1 us
  local copies, waits for them, and re-layouts: 4.71 us -> 0.42 us
    ppermute x25 -> x21, waiting for transfers between devices: 17 us -> 27.1 us  [send(): got = lax.ppermute(data, 'dp', STEPS[step])]
    pallas_call x6 -> x4, Pallas kernels: 22.1 us -> 13.8 us  [term(): pl.pallas_call(functools.partial(term_kernel, segments, plan, blocks), ou...]
    ppermute x25 -> x21, starting transfers between devices: 32 us -> 26 us  [send(): got = lax.ppermute(data, 'dp', STEPS[step])]
    ppermute x12, starting transfers between devices: 28.9 us -> 33.7 us  [layer_move(): return lax.ppermute(value, 'layer', pairs)]
    unnamed x7 -> x4, local copies, waits for them, and re-layouts: 3.41 us -> 0.01 us
    ppermute x12, waiting for transfers between devices: 11 us -> 9.06 us  [layer_move(): return lax.ppermute(value, 'layer', pairs)]
  transfers between devices with their start and end apart: 37 -> 33, of which waited for: 11 -> 12; matrix products, arithmetic and copies ran while one was open for 1% -> 1% of each run, Pallas kernels for 19% -> 12%
where the time goes in v2:
time: 114 us; the launch traced here: 113 us
  starting transfers between devices  59.7 us (52%)
  waiting for transfers between devices  36.1 us (32%)
  Pallas kernels  15 us (13%)
  other arithmetic  1.77 us (2%)
    ppermute x12, starting transfers between devices, layer_move(): return lax.ppermute(value, 'layer', pairs)  33.7 us
    ppermute x21, waiting for transfers between devices, send(): got = lax.ppermute(data, 'dp', STEPS[step])  27.1 us
    ppermute x21, starting transfers between devices, send(): got = lax.ppermute(data, 'dp', STEPS[step])  26 us
    pallas_call x4, Pallas kernels, term(): pl.pallas_call(functools.partial(term_kernel, segments, plan, blocks), ou...  13.8 us
    ppermute x12, waiting for transfers between devices, layer_move(): return lax.ppermute(value, 'layer', pairs)  9.06 us
  transfers between devices with their start and end apart: 33, of which 12 were waited for; matrix products, arithmetic and copies ran while one was open for 1% of the time, Pallas kernels for 12%

profile of v2, /device:TPU:1, one launch (start us, length us, event | category | flops | bytes accessed | tf_op | source)
XLA Modules:
  0.0 113.5 jit_solution(6200918240165618701)
XLA Ops:
  1.2 3.4 %collective-permute-start.7 = (bf16[32,4608]{1,0:T(8,128)(2,1)S(1)}, bf16[32,4608]{1,0:T(8,128)(2,1)S(1)}, u32[]{:S(2)}, u32[]{:S(2)}) collective-permute-start(bf16[32,4608]{1,0:T(8,128)(2,1)S(1)} %bitcast.37), channel_id=1, source_target_pairs={{0,48},{8,56},{16,0},{24,8},{32,16},{40,24},{48,32},{56,40},{64,11... | collective-permute-start | bytes 884744 | tf_op jit(solution)/shard_map/ppermute | solution.py:92
  4.5 2.7 %collective-permute-start.3 = (bf16[32,4608]{1,0:T(8,128)(2,1)S(1)}, bf16[32,4608]{1,0:T(8,128)(2,1)S(1)}, u32[]{:S(2)}, u32[]{:S(2)}) collective-permute-start(bf16[32,4608]{1,0:T(8,128)(2,1)S(1)} %bitcast.38), channel_id=1, source_target_pairs={{0,192},{8,200},{16,208},{24,216},{32,224},{40,232},{48,240},{56,2... | collective-permute-start | bytes 884744 | tf_op jit(solution)/shard_map/ppermute | solution.py:92
  7.3 1.6 %collective-permute-start = (bf16[32,4608]{1,0:T(8,128)(2,1)S(1)}, bf16[32,4608]{1,0:T(8,128)(2,1)S(1)}, u32[]{:S(2)}, u32[]{:S(2)}) collective-permute-start(bf16[32,4608]{1,0:T(8,128)(2,1)S(1)} %bitcast.41), channel_id=1, source_target_pairs={{0,8},{8,0},{16,24},{24,16},{32,40},{40,32},{48,56},{56,48},{64,72... | collective-permute-start | bytes 884744 | tf_op jit(solution)/shard_map/ppermute | solution.py:92
  8.9 1.3 %collective-permute-done.7.refs_2_ = bf16[32,4608]{1,0:T(8,128)(2,1)S(1)} collective-permute-done((bf16[32,4608]{1,0:T(8,128)(2,1)S(1)}, bf16[32,4608]{1,0:T(8,128)(2,1)S(1)}, u32[]{:S(2)}, u32[]{:S(2)}) %collective-permute-start.7) | collective-permute-done | bytes 294944 | tf_op jit(solution)/shard_map/ppermute | solution.py:92
  10.2 2.4 %collective-permute-done.3.refs_4_ = bf16[32,4608]{1,0:T(8,128)(2,1)S(1)} collective-permute-done((bf16[32,4608]{1,0:T(8,128)(2,1)S(1)}, bf16[32,4608]{1,0:T(8,128)(2,1)S(1)}, u32[]{:S(2)}, u32[]{:S(2)}) %collective-permute-start.3) | collective-permute-done | bytes 294944 | tf_op jit(solution)/shard_map/ppermute | solution.py:92
  12.7 3.1 %collective-permute-done.5.refs_3_ = bf16[32,4608]{1,0:T(8,128)(2,1)S(1)} collective-permute-done((bf16[32,4608]{1,0:T(8,128)(2,1)S(1)}, bf16[32,4608]{1,0:T(8,128)(2,1)S(1)}, u32[]{:S(2)}, u32[]{:S(2)}) %collective-permute-start.5) | collective-permute-done | bytes 294944 | tf_op jit(solution)/shard_map/ppermute | solution.py:92
  16.1 2.7 %collective-permute-start.4 = (bf16[48,4608]{1,0:T(8,128)(2,1)S(1)}, bf16[48,4608]{1,0:T(8,128)(2,1)S(1)}, u32[]{:S(2)}, u32[]{:S(2)}) collective-permute-start(bf16[48,4608]{1,0:T(8,128)(2,1)S(1)} %get-tuple-element.70), channel_id=1, source_target_pairs={{0,192},{8,200},{16,208},{24,216},{32,224},{40,232},{48,240},{56,2... | collective-permute-start | bytes 1327112 | tf_op jit(solution)/shard_map/ppermute | solution.py:92
  18.7 1.5 %collective-permute-start.8 = (bf16[48,4608]{1,0:T(8,128)(2,1)S(1)}, bf16[48,4608]{1,0:T(8,128)(2,1)S(1)}, u32[]{:S(2)}, u32[]{:S(2)}) collective-permute-start(bf16[48,4608]{1,0:T(8,128)(2,1)S(1)} %get-tuple-element.69), channel_id=1, source_target_pairs={{0,48},{8,56},{16,0},{24,8},{32,16},{40,24},{48,32},{56,40},{64,11... | collective-permute-start | bytes 1327112 | tf_op jit(solution)/shard_map/ppermute | solution.py:92
  20.2 7.4 %collective-permute-done.8.refs_6_ = bf16[48,4608]{1,0:T(8,128)(2,1)S(1)} collective-permute-done((bf16[48,4608]{1,0:T(8,128)(2,1)S(1)}, bf16[48,4608]{1,0:T(8,128)(2,1)S(1)}, u32[]{:S(2)}, u32[]{:S(2)}) %collective-permute-start.8) | collective-permute-done | bytes 442400 | tf_op jit(solution)/shard_map/ppermute | solution.py:92
  27.8 2.2 %collective-permute-done.2.refs_5_ = bf16[48,4608]{1,0:T(8,128)(2,1)S(1)} collective-permute-done((bf16[48,4608]{1,0:T(8,128)(2,1)S(1)}, bf16[48,4608]{1,0:T(8,128)(2,1)S(1)}, u32[]{:S(2)}, u32[]{:S(2)}) %collective-permute-start.2) | collective-permute-done | bytes 442400 | tf_op jit(solution)/shard_map/ppermute | solution.py:92
  30.8 2.7 %collective-permute-start.10 = (bf16[48,4608]{1,0:T(8,128)(2,1)S(1)}, bf16[48,4608]{1,0:T(8,128)(2,1)S(1)}, u32[]{:S(2)}, u32[]{:S(2)}) collective-permute-start(bf16[48,4608]{1,0:T(8,128)(2,1)S(1)} %get-tuple-element.67), channel_id=1, source_target_pairs={{0,192},{8,200},{16,208},{24,216},{32,224},{40,232},{48,240},{56,2... | collective-permute-start | bytes 1327112 | tf_op jit(solution)/shard_map/ppermute | solution.py:92
  34.5 3.5 %shard_map.46 = f32[2,32,1024]{2,1,0:T(8,128)S(1)} custom-call(bf16[1024,4096]{1,0:T(8,128)(2,1)S(1)} %bitcast.29, bf16[1024,512]{1,0:T(8,128)(2,1)S(1)} %bitcast.33, bf16[32,4608]{1,0:T(8,128)(2,1)S(1)} %collective-permute-done.refs_0_, bf16[32,4608]{1,0:T(8,128)(2,1)S(1)} %collective-permute-done.1.refs_1_, ...), custom_call_target="tpu_custom_call" | custom-call | flops 2415919104 | bytes 1 | tf_op jit(solution)/shard_map/pallas_call | solution.py:152
  38.1 1.5 %collective-permute-done.11.refs_3_ = bf16[48,4608]{1,0:T(8,128)(2,1)S(1)} collective-permute-done((bf16[48,4608]{1,0:T(8,128)(2,1)S(1)}, bf16[48,4608]{1,0:T(8,128)(2,1)S(1)}, u32[]{:S(2)}, u32[]{:S(2)}) %collective-permute-start.11) | collective-permute-done | bytes 442400 | tf_op jit(solution)/shard_map/ppermute | solution.py:92
  39.6 1.4 %collective-permute-start.14 = (bf16[64,4608]{1,0:T(8,128)(2,1)S(1)}, bf16[64,4608]{1,0:T(8,128)(2,1)S(1)}, u32[]{:S(2)}, u32[]{:S(2)}) collective-permute-start(bf16[64,4608]{1,0:T(8,128)(2,1)S(1)} %pad_maximum_fusion.6), channel_id=1, source_target_pairs={{0,192},{8,200},{16,208},{24,216},{32,224},{40,232},{48,240},{56,2... | collective-permute-start | bytes 1769480 | tf_op jit(solution)/shard_map/ppermute | solution.py:92
  41.1 6.7 %collective-permute-start.9 = (f32[32,1024]{1,0:T(8,128)S(1)}, f32[32,1024]{1,0:T(8,128)S(1)}, u32[]{:S(2)}, u32[]{:S(2)}) collective-permute-start(f32[32,1024]{1,0:T(8,128)S(1)} %slice_bitcast_fusion.6), channel_id=1, source_target_pairs={{0,1},{1,0},{2,3},{3,2},{4,5},{5,4},{6,7},{7,6},{8,9},{9,8},{10,11... | collective-permute-start | bytes 393224 | tf_op jit(solution)/shard_map/ppermute | solution.py:170
  47.8 5.5 %collective-permute-done.13.refs_2_ = bf16[64,4608]{1,0:T(8,128)(2,1)S(1)} collective-permute-done((bf16[64,4608]{1,0:T(8,128)(2,1)S(1)}, bf16[64,4608]{1,0:T(8,128)(2,1)S(1)}, u32[]{:S(2)}, u32[]{:S(2)}) %collective-permute-start.13) | collective-permute-done | bytes 589856 | tf_op jit(solution)/shard_map/ppermute | solution.py:92
  53.7 5.4 %collective-permute-start.16 = (f32[32,1024]{1,0:T(8,128)S(1)}, f32[32,1024]{1,0:T(8,128)S(1)}, u32[]{:S(2)}, u32[]{:S(2)}) collective-permute-start(f32[32,1024]{1,0:T(8,128)S(1)} %fusion.1), channel_id=1, source_target_pairs={{0,2},{1,7},{2,0},{3,5},{4,6},{5,3},{6,4},{7,1},{8,10},{9,15},{10,... | collective-permute-start | bytes 393224 | tf_op jit(solution)/shard_map/ppermute | solution.py:170
  59.1 1.5 %collective-permute-start.20 = (bf16[64,4608]{1,0:T(8,128)(2,1)S(1)}, bf16[64,4608]{1,0:T(8,128)(2,1)S(1)}, u32[]{:S(2)}, u32[]{:S(2)}) collective-permute-start(bf16[64,4608]{1,0:T(8,128)(2,1)S(1)} %get-tuple-element.28), channel_id=1, source_target_pairs={{0,16},{8,24},{16,32},{24,40},{32,48},{40,56},{48,0},{56,8},{64,80... | collective-permute-start | bytes 1769480 | tf_op jit(solution)/shard_map/ppermute | solution.py:92
  61.8 3.4 %shard_map.47 = f32[2,32,1024]{2,1,0:T(8,128)S(1)} custom-call(bf16[1024,4096]{1,0:T(8,128)(2,1)S(1)} %bitcast.30, bf16[1024,512]{1,0:T(8,128)(2,1)S(1)} %bitcast.34, bf16[32,4608]{1,0:T(8,128)(2,1)S(1)} %bitcast.42, bf16[48,4608]{1,0:T(8,128)(2,1)S(1)} %collective-permute-done.6.refs_1_, bf16[48,4608]{1,0:T(8,128)(2,1)S(1)} %collective-permute-done.4.refs_2_, ...), custom_call_target="tpu_custom_call" | custom-call | flops 2415919104 | bytes 1 | tf_op jit(solution)/shard_map/pallas_call | solution.py:152
  65.3 3.4 %shard_map.48 = f32[2,32,1024]{2,1,0:T(8,128)S(1)} custom-call(bf16[1024,4096]{1,0:T(8,128)(2,1)S(1)} %bitcast.31, bf16[1024,512]{1,0:T(8,128)(2,1)S(1)} %bitcast.35, bf16[80,4608]{1,0:T(8,128)(2,1)S(1)} %collective-permute-done.12.refs_5_.refs_0_, bf16[80,4608]{1,0:T(8,128)(2,1)S(1)} %collective-permute-done.15.refs_6_.refs_1_, ...), custom_call_target="tpu_custom_call" | custom-call | flops 2415919104 | bytes 1 | tf_op jit(solution)/shard_map/pallas_call | solution.py:152
  68.8 2.4 %collective-permute-start.19 = (f32[64,1024]{1,0:T(8,128)S(1)}, f32[64,1024]{1,0:T(8,128)S(1)}, u32[]{:S(2)}, u32[]{:S(2)}) collective-permute-start(f32[64,1024]{1,0:T(8,128)S(1)} %pad_maximum_fusion.18), channel_id=1, source_target_pairs={{0,1},{1,0},{2,3},{3,2},{4,5},{5,4},{6,7},{7,6},{8,9},{9,8},{10,11... | collective-permute-start | bytes 786440 | tf_op jit(solution)/shard_map/ppermute | solution.py:170
  71.2 2.8 %collective-permute-start.24 = (bf16[48,4608]{1,0:T(8,128)(2,1)S(1)}, bf16[48,4608]{1,0:T(8,128)(2,1)S(1)}, u32[]{:S(2)}, u32[]{:S(2)}) collective-permute-start(bf16[48,4608]{1,0:T(8,128)(2,1)S(1)} %pad_maximum_fusion.17), channel_id=1, source_target_pairs={{0,192},{8,200},{16,208},{24,216},{32,224},{40,232},{48,240},{56,2... | collective-permute-start | bytes 1327112 | tf_op jit(solution)/shard_map/ppermute | solution.py:92
  74.4 2.4 %collective-permute-start.26 = (bf16[16,4608]{1,0:T(8,128)(2,1)S(1)}, bf16[16,4608]{1,0:T(8,128)(2,1)S(1)}, u32[]{:S(2)}, u32[]{:S(2)}) collective-permute-start(bf16[16,4608]{1,0:T(8,128)(2,1)S(1)} %slice.173), channel_id=1, source_target_pairs={{0,48},{8,56},{16,0},{24,8},{32,16},{40,24},{48,32},{56,40},{64,11... | collective-permute-start | bytes 442376 | tf_op jit(solution)/shard_map/ppermute | solution.py:92
  76.8 3.9 %collective-permute-start.22 = (f32[64,1024]{1,0:T(8,128)S(1)}, f32[64,1024]{1,0:T(8,128)S(1)}, u32[]{:S(2)}, u32[]{:S(2)}) collective-permute-start(f32[64,1024]{1,0:T(8,128)S(1)} %maximum_add_fusion), channel_id=1, source_target_pairs={{0,2},{1,7},{2,0},{3,5},{4,6},{5,3},{6,4},{7,1},{8,10},{9,15},{10,... | collective-permute-start | bytes 786440 | tf_op jit(solution)/shard_map/ppermute | solution.py:170
  80.7 3.6 %collective-permute-done.23.refs_2_ = bf16[48,4608]{1,0:T(8,128)(2,1)S(1)} collective-permute-done((bf16[48,4608]{1,0:T(8,128)(2,1)S(1)}, bf16[48,4608]{1,0:T(8,128)(2,1)S(1)}, u32[]{:S(2)}, u32[]{:S(2)}) %collective-permute-start.23) | collective-permute-done | bytes 442400 | tf_op jit(solution)/shard_map/ppermute | solution.py:92
  84.3 3.4 %shard_map.49 = f32[2,32,1024]{2,1,0:T(8,128)S(1)} custom-call(bf16[1024,4096]{1,0:T(8,128)(2,1)S(1)} %bitcast.32, bf16[1024,512]{1,0:T(8,128)(2,1)S(1)} %bitcast.36, bf16[64,4608]{1,0:T(8,128)(2,1)S(1)} %collective-permute-done.20.refs_0_, bf16[64,4608]{1,0:T(8,128)(2,1)S(1)} %collective-permute-done.21.refs_1_, ...), custom_call_target="tpu_custom_call" | custom-call | flops 2415919104 | bytes 1 | tf_op jit(solution)/shard_map/pallas_call | solution.py:152
  89.7 4.2 %collective-permute-start.30 = (f32[32,1024]{1,0:T(8,128)S(1)}, f32[32,1024]{1,0:T(8,128)S(1)}, u32[]{:S(2)}, u32[]{:S(2)}) collective-permute-start(f32[32,1024]{1,0:T(8,128)S(1)} %fusion), channel_id=1, source_target_pairs={{0,2},{1,7},{2,0},{3,5},{4,6},{5,3},{6,4},{7,1},{8,10},{9,15},{10,... | collective-permute-start | bytes 393224 | tf_op jit(solution)/shard_map/ppermute | solution.py:170
  95.0 6.7 %collective-permute-done.27 = f32[64,1024]{1,0:T(8,128)S(1)} collective-permute-done((f32[64,1024]{1,0:T(8,128)S(1)}, f32[64,1024]{1,0:T(8,128)S(1)}, u32[]{:S(2)}, u32[]{:S(2)}) %collective-permute-start.27) | collective-permute-done | bytes 262176 | tf_op jit(solution)/shard_map/ppermute | solution.py:170
  101.8 2.8 %collective-permute-start.31 = (f32[32,1024]{1,0:T(8,128)S(1)}, f32[32,1024]{1,0:T(8,128)S(1)}, u32[]{:S(2)}, u32[]{:S(2)}) collective-permute-start(f32[32,1024]{1,0:T(8,128)S(1)} %add.34), channel_id=1, source_target_pairs={{0,6},{1,3},{2,4},{3,1},{4,2},{5,7},{6,0},{7,5},{8,14},{9,11},{10,... | collective-permute-start | bytes 393224 | tf_op jit(solution)/shard_map/ppermute | solution.py:170
  104.6 2.6 %collective-permute-start.29 = (f32[64,1024]{1,0:T(8,128)S(1)}, f32[64,1024]{1,0:T(8,128)S(1)}, u32[]{:S(2)}, u32[]{:S(2)}) collective-permute-start(f32[64,1024]{1,0:T(8,128)S(1)} %add.33.refs_2_), channel_id=1, source_target_pairs={{0,1},{1,0},{2,3},{3,2},{4,5},{5,4},{6,7},{7,6},{8,9},{9,8},{10,11... | collective-permute-start | bytes 786440 | tf_op jit(solution)/shard_map/ppermute | solution.py:170
  108.3 2.9 %collective-permute-start.32 = (f32[32,1024]{1,0:T(8,128)S(1)}, f32[32,1024]{1,0:T(8,128)S(1)}, u32[]{:S(2)}, u32[]{:S(2)}) collective-permute-start(f32[32,1024]{1,0:T(8,128)S(1)} %add.35.refs_4_), channel_id=1, source_target_pairs={{0,1},{1,0},{2,3},{3,2},{4,5},{5,4},{6,7},{7,6},{8,9},{9,8},{10,11... | collective-permute-start | bytes 393224 | tf_op jit(solution)/shard_map/ppermute | solution.py:170
  112.2 1.2 %shard_map.50 = f32[256,1024]{1,0:T(8,128)} custom-call(f32[32,1024]{1,0:T(8,128)S(1)} %add.29.refs_0_, f32[32,1024]{1,0:T(8,128)S(1)} %collective-permute-done.18.refs_1_, f32[64,1024]{1,0:T(8,128)S(1)} %add.33.refs_2_, f32[64,1024]{1,0:T(8,128)S(1)} %collective-permute-done.29.refs_3_, f32[32,1024]{1,0:T(8,128)S(1)} %add.35.refs_4_, ...), custom_call_target="tpu_custom_call" | custom-call | tf_op jit(solution)/shard_map/pallas_call | solution.py:197
  (84 shorter events, 10.7 us)
Async XLA Ops:
  1.2 9.1 %collective-permute-start.7 = (bf16[32,4608]{1,0:T(8,128)(2,1)S(1)}, bf16[32,4608]{1,0:T(8,128)(2,1)S(1)}, u32[]{:S(2)}, u32[]{:S(2)}) collective-permute-start(bf16[32,4608]{1,0:T(8,128)(2,1)S(1)} %bitcast.37), channel_id=1, source_target_pairs={{0,48},{8,56},{16,0},{24,8},{32,16},{40,24},{48,32},{56,40},{64,11... | collective-permute-start | bytes 884744 | tf_op jit(solution)/shard_map/ppermute | solution.py:92
  4.5 8.1 %collective-permute-start.3 = (bf16[32,4608]{1,0:T(8,128)(2,1)S(1)}, bf16[32,4608]{1,0:T(8,128)(2,1)S(1)}, u32[]{:S(2)}, u32[]{:S(2)}) collective-permute-start(bf16[32,4608]{1,0:T(8,128)(2,1)S(1)} %bitcast.38), channel_id=1, source_target_pairs={{0,192},{8,200},{16,208},{24,216},{32,224},{40,232},{48,240},{56,2... | collective-permute-start | bytes 884744 | tf_op jit(solution)/shard_map/ppermute | solution.py:92
  7.3 8.5 %collective-permute-start.5 = (bf16[32,4608]{1,0:T(8,128)(2,1)S(1)}, bf16[32,4608]{1,0:T(8,128)(2,1)S(1)}, u32[]{:S(2)}, u32[]{:S(2)}) collective-permute-start(bf16[32,4608]{1,0:T(8,128)(2,1)S(1)} %bitcast.39), channel_id=1, source_target_pairs={{0,64},{8,72},{16,80},{24,88},{32,96},{40,104},{48,112},{56,120},{... | collective-permute-start | bytes 884744 | tf_op jit(solution)/shard_map/ppermute | solution.py:92
  7.3 8.5 %collective-permute-start.1 = (bf16[32,4608]{1,0:T(8,128)(2,1)S(1)}, bf16[32,4608]{1,0:T(8,128)(2,1)S(1)}, u32[]{:S(2)}, u32[]{:S(2)}) collective-permute-start(bf16[32,4608]{1,0:T(8,128)(2,1)S(1)} %bitcast.40), channel_id=1, source_target_pairs={{0,16},{8,24},{16,32},{24,40},{32,48},{40,56},{48,0},{56,8},{64,80... | collective-permute-start | bytes 884744 | tf_op jit(solution)/shard_map/ppermute | solution.py:92
  7.3 8.5 %collective-permute-start = (bf16[32,4608]{1,0:T(8,128)(2,1)S(1)}, bf16[32,4608]{1,0:T(8,128)(2,1)S(1)}, u32[]{:S(2)}, u32[]{:S(2)}) collective-permute-start(bf16[32,4608]{1,0:T(8,128)(2,1)S(1)} %bitcast.41), channel_id=1, source_target_pairs={{0,8},{8,0},{16,24},{24,16},{32,40},{40,32},{48,56},{56,48},{64,72... | collective-permute-start | bytes 884744 | tf_op jit(solution)/shard_map/ppermute | solution.py:92
  16.0 11.7 %collective-permute-start.6 = (bf16[48,4608]{1,0:T(8,128)(2,1)S(1)}, bf16[48,4608]{1,0:T(8,128)(2,1)S(1)}, u32[]{:S(2)}, u32[]{:S(2)}) collective-permute-start(bf16[48,4608]{1,0:T(8,128)(2,1)S(1)} %get-tuple-element.71), channel_id=1, source_target_pairs={{0,64},{8,72},{16,80},{24,88},{32,96},{40,104},{48,112},{56,120},{... | collective-permute-start | bytes 1327112 | tf_op jit(solution)/shard_map/ppermute | solution.py:92
  16.1 11.7 %collective-permute-start.4 = (bf16[48,4608]{1,0:T(8,128)(2,1)S(1)}, bf16[48,4608]{1,0:T(8,128)(2,1)S(1)}, u32[]{:S(2)}, u32[]{:S(2)}) collective-permute-start(bf16[48,4608]{1,0:T(8,128)(2,1)S(1)} %get-tuple-element.70), channel_id=1, source_target_pairs={{0,192},{8,200},{16,208},{24,216},{32,224},{40,232},{48,240},{56,2... | collective-permute-start | bytes 1327112 | tf_op jit(solution)/shard_map/ppermute | solution.py:92
  18.7 8.9 %collective-permute-start.8 = (bf16[48,4608]{1,0:T(8,128)(2,1)S(1)}, bf16[48,4608]{1,0:T(8,128)(2,1)S(1)}, u32[]{:S(2)}, u32[]{:S(2)}) collective-permute-start(bf16[48,4608]{1,0:T(8,128)(2,1)S(1)} %get-tuple-element.69), channel_id=1, source_target_pairs={{0,48},{8,56},{16,0},{24,8},{32,16},{40,24},{48,32},{56,40},{64,11... | collective-permute-start | bytes 1327112 | tf_op jit(solution)/shard_map/ppermute | solution.py:92
  20.2 9.8 %collective-permute-start.2 = (bf16[48,4608]{1,0:T(8,128)(2,1)S(1)}, bf16[48,4608]{1,0:T(8,128)(2,1)S(1)}, u32[]{:S(2)}, u32[]{:S(2)}) collective-permute-start(bf16[48,4608]{1,0:T(8,128)(2,1)S(1)} %get-tuple-element.72), channel_id=1, source_target_pairs={{0,16},{8,24},{16,32},{24,40},{32,48},{40,56},{48,0},{56,8},{64,80... | collective-permute-start | bytes 1327112 | tf_op jit(solution)/shard_map/ppermute | solution.py:92
  30.1 23.4 %collective-permute-start.15 = (bf16[80,4608]{1,0:T(8,128)(2,1)S(1)}, bf16[80,4608]{1,0:T(8,128)(2,1)S(1)}, u32[]{:S(2)}, u32[]{:S(2)}) collective-permute-start(bf16[80,4608]{1,0:T(8,128)(2,1)S(1)} %get-tuple-element.55), channel_id=1, source_target_pairs={{0,48},{8,56},{16,0},{24,8},{32,16},{40,24},{48,32},{56,40},{64,11... | collective-permute-start | bytes 2211848 | tf_op jit(solution)/shard_map/ppermute | solution.py:92
  30.7 8.9 %collective-permute-start.11 = (bf16[48,4608]{1,0:T(8,128)(2,1)S(1)}, bf16[48,4608]{1,0:T(8,128)(2,1)S(1)}, u32[]{:S(2)}, u32[]{:S(2)}) collective-permute-start(bf16[48,4608]{1,0:T(8,128)(2,1)S(1)} %get-tuple-element.68), channel_id=1, source_target_pairs={{0,64},{8,72},{16,80},{24,88},{32,96},{40,104},{48,112},{56,120},{... | collective-permute-start | bytes 1327112 | tf_op jit(solution)/shard_map/ppermute | solution.py:92
  30.8 10.3 %collective-permute-start.10 = (bf16[48,4608]{1,0:T(8,128)(2,1)S(1)}, bf16[48,4608]{1,0:T(8,128)(2,1)S(1)}, u32[]{:S(2)}, u32[]{:S(2)}) collective-permute-start(bf16[48,4608]{1,0:T(8,128)(2,1)S(1)} %get-tuple-element.67), channel_id=1, source_target_pairs={{0,192},{8,200},{16,208},{24,216},{32,224},{40,232},{48,240},{56,2... | collective-permute-start | bytes 1327112 | tf_op jit(solution)/shard_map/ppermute | solution.py:92
  33.4 20.1 %collective-permute-start.12 = (bf16[80,4608]{1,0:T(8,128)(2,1)S(1)}, bf16[80,4608]{1,0:T(8,128)(2,1)S(1)}, u32[]{:S(2)}, u32[]{:S(2)}) collective-permute-start(bf16[80,4608]{1,0:T(8,128)(2,1)S(1)} %get-tuple-element.56), channel_id=1, source_target_pairs={{0,16},{8,24},{16,32},{24,40},{32,48},{40,56},{48,0},{56,8},{64,80... | collective-permute-start | bytes 2211848 | tf_op jit(solution)/shard_map/ppermute | solution.py:92
  38.0 15.3 %collective-permute-start.13 = (bf16[64,4608]{1,0:T(8,128)(2,1)S(1)}, bf16[64,4608]{1,0:T(8,128)(2,1)S(1)}, u32[]{:S(2)}, u32[]{:S(2)}) collective-permute-start(bf16[64,4608]{1,0:T(8,128)(2,1)S(1)} %pad_maximum_fusion.6), channel_id=1, source_target_pairs={{0,64},{8,72},{16,80},{24,88},{32,96},{40,104},{48,112},{56,120},{... | collective-permute-start | bytes 1769480 | tf_op jit(solution)/shard_map/ppermute | solution.py:92
  39.6 13.7 %collective-permute-start.14 = (bf16[64,4608]{1,0:T(8,128)(2,1)S(1)}, bf16[64,4608]{1,0:T(8,128)(2,1)S(1)}, u32[]{:S(2)}, u32[]{:S(2)}) collective-permute-start(bf16[64,4608]{1,0:T(8,128)(2,1)S(1)} %pad_maximum_fusion.6), channel_id=1, source_target_pairs={{0,192},{8,200},{16,208},{24,216},{32,224},{40,232},{48,240},{56,2... | collective-permute-start | bytes 1769480 | tf_op jit(solution)/shard_map/ppermute | solution.py:92
  41.1 12.6 %collective-permute-start.9 = (f32[32,1024]{1,0:T(8,128)S(1)}, f32[32,1024]{1,0:T(8,128)S(1)}, u32[]{:S(2)}, u32[]{:S(2)}) collective-permute-start(f32[32,1024]{1,0:T(8,128)S(1)} %slice_bitcast_fusion.6), channel_id=1, source_target_pairs={{0,1},{1,0},{2,3},{3,2},{4,5},{5,4},{6,7},{7,6},{8,9},{9,8},{10,11... | collective-permute-start | bytes 393224 | tf_op jit(solution)/shard_map/ppermute | solution.py:170
  53.7 11.6 %collective-permute-start.16 = (f32[32,1024]{1,0:T(8,128)S(1)}, f32[32,1024]{1,0:T(8,128)S(1)}, u32[]{:S(2)}, u32[]{:S(2)}) collective-permute-start(f32[32,1024]{1,0:T(8,128)S(1)} %fusion.1), channel_id=1, source_target_pairs={{0,2},{1,7},{2,0},{3,5},{4,6},{5,3},{6,4},{7,1},{8,10},{9,15},{10,... | collective-permute-start | bytes 393224 | tf_op jit(solution)/shard_map/ppermute | solution.py:170
  59.1 14.8 %collective-permute-start.20 = (bf16[64,4608]{1,0:T(8,128)(2,1)S(1)}, bf16[64,4608]{1,0:T(8,128)(2,1)S(1)}, u32[]{:S(2)}, u32[]{:S(2)}) collective-permute-start(bf16[64,4608]{1,0:T(8,128)(2,1)S(1)} %get-tuple-element.28), channel_id=1, source_target_pairs={{0,16},{8,24},{16,32},{24,40},{32,48},{40,56},{48,0},{56,8},{64,80... | collective-permute-start | bytes 1769480 | tf_op jit(solution)/shard_map/ppermute | solution.py:92
  60.6 13.4 %collective-permute-start.21 = (bf16[64,4608]{1,0:T(8,128)(2,1)S(1)}, bf16[64,4608]{1,0:T(8,128)(2,1)S(1)}, u32[]{:S(2)}, u32[]{:S(2)}) collective-permute-start(bf16[64,4608]{1,0:T(8,128)(2,1)S(1)} %get-tuple-element.29), channel_id=1, source_target_pairs={{0,48},{8,56},{16,0},{24,8},{32,16},{40,24},{48,32},{56,40},{64,11... | collective-permute-start | bytes 1769480 | tf_op jit(solution)/shard_map/ppermute | solution.py:92
  68.8 8.0 %collective-permute-start.19 = (f32[64,1024]{1,0:T(8,128)S(1)}, f32[64,1024]{1,0:T(8,128)S(1)}, u32[]{:S(2)}, u32[]{:S(2)}) collective-permute-start(f32[64,1024]{1,0:T(8,128)S(1)} %pad_maximum_fusion.18), channel_id=1, source_target_pairs={{0,1},{1,0},{2,3},{3,2},{4,5},{5,4},{6,7},{7,6},{8,9},{9,8},{10,11... | collective-permute-start | bytes 786440 | tf_op jit(solution)/shard_map/ppermute | solution.py:170
  71.2 13.1 %collective-permute-start.23 = (bf16[48,4608]{1,0:T(8,128)(2,1)S(1)}, bf16[48,4608]{1,0:T(8,128)(2,1)S(1)}, u32[]{:S(2)}, u32[]{:S(2)}) collective-permute-start(bf16[48,4608]{1,0:T(8,128)(2,1)S(1)} %pad_maximum_fusion.16), channel_id=1, source_target_pairs={{0,64},{8,72},{16,80},{24,88},{32,96},{40,104},{48,112},{56,120},{... | collective-permute-start | bytes 1327112 | tf_op jit(solution)/shard_map/ppermute | solution.py:92
  71.2 13.1 %collective-permute-start.24 = (bf16[48,4608]{1,0:T(8,128)(2,1)S(1)}, bf16[48,4608]{1,0:T(8,128)(2,1)S(1)}, u32[]{:S(2)}, u32[]{:S(2)}) collective-permute-start(bf16[48,4608]{1,0:T(8,128)(2,1)S(1)} %pad_maximum_fusion.17), channel_id=1, source_target_pairs={{0,192},{8,200},{16,208},{24,216},{32,224},{40,232},{48,240},{56,2... | collective-permute-start | bytes 1327112 | tf_op jit(solution)/shard_map/ppermute | solution.py:92
  74.0 10.3 %collective-permute-start.25 = (bf16[16,4608]{1,0:T(8,128)(2,1)S(1)}, bf16[16,4608]{1,0:T(8,128)(2,1)S(1)}, u32[]{:S(2)}, u32[]{:S(2)}) collective-permute-start(bf16[16,4608]{1,0:T(8,128)(2,1)S(1)} %slice.172), channel_id=1, source_target_pairs={{0,16},{8,24},{16,32},{24,40},{32,48},{40,56},{48,0},{56,8},{64,80... | collective-permute-start | bytes 442376 | tf_op jit(solution)/shard_map/ppermute | solution.py:92
  74.4 9.9 %collective-permute-start.26 = (bf16[16,4608]{1,0:T(8,128)(2,1)S(1)}, bf16[16,4608]{1,0:T(8,128)(2,1)S(1)}, u32[]{:S(2)}, u32[]{:S(2)}) collective-permute-start(bf16[16,4608]{1,0:T(8,128)(2,1)S(1)} %slice.173), channel_id=1, source_target_pairs={{0,48},{8,56},{16,0},{24,8},{32,16},{40,24},{48,32},{56,40},{64,11... | collective-permute-start | bytes 442376 | tf_op jit(solution)/shard_map/ppermute | solution.py:92
  76.8 11.9 %collective-permute-start.22 = (f32[64,1024]{1,0:T(8,128)S(1)}, f32[64,1024]{1,0:T(8,128)S(1)}, u32[]{:S(2)}, u32[]{:S(2)}) collective-permute-start(f32[64,1024]{1,0:T(8,128)S(1)} %maximum_add_fusion), channel_id=1, source_target_pairs={{0,2},{1,7},{2,0},{3,5},{4,6},{5,3},{6,4},{7,1},{8,10},{9,15},{10,... | collective-permute-start | bytes 786440 | tf_op jit(solution)/shard_map/ppermute | solution.py:170
  88.7 13.1 %collective-permute-start.27 = (f32[64,1024]{1,0:T(8,128)S(1)}, f32[64,1024]{1,0:T(8,128)S(1)}, u32[]{:S(2)}, u32[]{:S(2)}) collective-permute-start(f32[64,1024]{1,0:T(8,128)S(1)} %add.31), channel_id=1, source_target_pairs={{0,6},{1,3},{2,4},{3,1},{4,2},{5,7},{6,0},{7,5},{8,14},{9,11},{10,... | collective-permute-start | bytes 786440 | tf_op jit(solution)/shard_map/ppermute | solution.py:170
  89.7 12.1 %collective-permute-start.30 = (f32[32,1024]{1,0:T(8,128)S(1)}, f32[32,1024]{1,0:T(8,128)S(1)}, u32[]{:S(2)}, u32[]{:S(2)}) collective-permute-start(f32[32,1024]{1,0:T(8,128)S(1)} %fusion), channel_id=1, source_target_pairs={{0,2},{1,7},{2,0},{3,5},{4,6},{5,3},{6,4},{7,1},{8,10},{9,15},{10,... | collective-permute-start | bytes 393224 | tf_op jit(solution)/shard_map/ppermute | solution.py:170
  93.8 13.4 %collective-permute-start.17 = (f32[32,1024]{1,0:T(8,128)S(1)}, f32[32,1024]{1,0:T(8,128)S(1)}, u32[]{:S(2)}, u32[]{:S(2)}) collective-permute-start(f32[32,1024]{1,0:T(8,128)S(1)} %add.28), channel_id=1, source_target_pairs={{0,6},{1,3},{2,4},{3,1},{4,2},{5,7},{6,0},{7,5},{8,14},{9,11},{10,... | collective-permute-start | bytes 393224 | tf_op jit(solution)/shard_map/ppermute | solution.py:170
  101.8 6.5 %collective-permute-start.31 = (f32[32,1024]{1,0:T(8,128)S(1)}, f32[32,1024]{1,0:T(8,128)S(1)}, u32[]{:S(2)}, u32[]{:S(2)}) collective-permute-start(f32[32,1024]{1,0:T(8,128)S(1)} %add.34), channel_id=1, source_target_pairs={{0,6},{1,3},{2,4},{3,1},{4,2},{5,7},{6,0},{7,5},{8,14},{9,11},{10,... | collective-permute-start | bytes 393224 | tf_op jit(solution)/shard_map/ppermute | solution.py:170
  104.6 6.7 %collective-permute-start.29 = (f32[64,1024]{1,0:T(8,128)S(1)}, f32[64,1024]{1,0:T(8,128)S(1)}, u32[]{:S(2)}, u32[]{:S(2)}) collective-permute-start(f32[64,1024]{1,0:T(8,128)S(1)} %add.33.refs_2_), channel_id=1, source_target_pairs={{0,1},{1,0},{2,3},{3,2},{4,5},{5,4},{6,7},{7,6},{8,9},{9,8},{10,11... | collective-permute-start | bytes 786440 | tf_op jit(solution)/shard_map/ppermute | solution.py:170
  107.3 4.0 %collective-permute-start.18 = (f32[32,1024]{1,0:T(8,128)S(1)}, f32[32,1024]{1,0:T(8,128)S(1)}, u32[]{:S(2)}, u32[]{:S(2)}) collective-permute-start(f32[32,1024]{1,0:T(8,128)S(1)} %add.29.refs_0_), channel_id=1, source_target_pairs={{0,1},{1,0},{2,3},{3,2},{4,5},{5,4},{6,7},{7,6},{8,9},{9,8},{10,11... | collective-permute-start | bytes 393224 | tf_op jit(solution)/shard_map/ppermute | solution.py:170
  108.3 3.9 %collective-permute-start.32 = (f32[32,1024]{1,0:T(8,128)S(1)}, f32[32,1024]{1,0:T(8,128)S(1)}, u32[]{:S(2)}, u32[]{:S(2)}) collective-permute-start(f32[32,1024]{1,0:T(8,128)S(1)} %add.35.refs_4_), channel_id=1, source_target_pairs={{0,1},{1,0},{2,3},{3,2},{4,5},{5,4},{6,7},{7,6},{8,9},{9,8},{10,11... | collective-permute-start | bytes 393224 | tf_op jit(solution)/shard_map/ppermute | solution.py:170
  (3 other events, 25.0 us)
